TPU v7x, 32 devices: a whole 2x2x4 slice. The times are simulated.
32 devices in a mesh: groups: 2 (over y), ex: 4 (over z), layer: 4 (over x, core).
Axes of the slice: x: 2, y: 2, z: 4, core: 2. Of those that a mesh axis runs over, the one named last changes fastest.
Arguments:
- layer_inputs: bfloat16 [4, 1024, 1280], P('layer', ('groups', 'ex')), parts along dimension 1, may hold values from -6 to 6
- out_grads: bfloat16 [4, 1024, 5120], P('layer', ('groups', 'ex')), parts along dimension 1, may hold values from -6 to 6
- proj_in: bfloat16 [4, 1280, 32], P('layer'), may hold values from -0.15625 to 0.15625
- proj_out: bfloat16 [4, 5120, 32], P('layer'), may hold values from -0.078125 to 0.078125
- frame_lengths: int32 [8, 16], P(('groups', 'ex')), parts along dimension 0, may hold values from 1 to 32, 128 in all within a row
- query_ids: int32 [512], P('groups'), parts along dimension 0, may hold values from 0 to 63
Outputs:
- scores: float32 [512, 64], P('groups', 'ex'), parts along dimension 0
There are 2 independent parts, one for each index of `groups`. A program takes and returns all parts, laid end to end along the dimension named above; an argument that names none is the same for every part. Nothing has to cross between parts.
Inputs may be any that keep to these rules, and one draw needn't show every extreme that they name: `frame_lengths`: each row fills the 128 frames of one index of ex.
All inputs are finite; a program needn't handle non-finite values.
Results may differ from a plain program's by a relative error of at most 0.0003.
Values sent between devices are 32-bit elements; how exact they have to be, the bound alone decides.
No kernel may reach another device: no remote copies, remote signals or barrier semaphores. Data moves between devices by JAX's collectives and lax.ppermute only.
A program may use at most 64 MiB of HBM per device.

v0:
```python
import jax
import jax.numpy as jnp
from jax import lax
from jax.sharding import PartitionSpec as P


def per_device(layer_inputs, out_grads, proj_in, proj_out, frame_lengths, query_ids):
    frame_count = layer_inputs.shape[1]
    in_proj = jnp.dot(layer_inputs[0], proj_in[0], preferred_element_type=jnp.float32)
    out_proj = jnp.dot(out_grads[0], proj_out[0], preferred_element_type=jnp.float32)
    rank = in_proj.shape[1]
    width = rank * rank
    outer_terms = (out_proj[:, :, None] * in_proj[:, None, :]).reshape(frame_count, width)
    lengths = frame_lengths[0]
    end_frames = jnp.cumsum(lengths)
    starts = end_frames - lengths
    positions = jnp.arange(frame_count, dtype=jnp.int32)
    member = (
        (positions[None, :] >= starts[:, None]) & (positions[None, :] < end_frames[:, None])
    ).astype(jnp.float32)
    features = jnp.dot(member, outer_terms, precision=lax.Precision.HIGHEST)
    all_features = lax.all_gather(features, "ex", axis=0, tiled=True)
    total_examples = all_features.shape[0]
    example_ids = jnp.arange(total_examples, dtype=jnp.int32)
    chosen = (query_ids[:, None] == example_ids[None, :]).astype(jnp.float32)
    queries = jnp.dot(chosen, all_features, precision=lax.Precision.HIGHEST)
    partial_gram = jnp.dot(features.T, features, precision=lax.Precision.HIGHEST)
    gram_rows = lax.psum_scatter(partial_gram, "ex", scatter_dimension=0, tiled=True)
    gram_matrix = lax.all_gather(gram_rows, "ex", axis=0, tiled=True)
    damping = 0.1 * jnp.trace(gram_matrix) / width
    factor = jnp.linalg.cholesky(gram_matrix + damping * jnp.eye(width, dtype=jnp.float32))
    precond = jax.scipy.linalg.cho_solve((factor, True), queries.T).T
    local_scores = jnp.dot(precond, features.T, precision=lax.Precision.HIGHEST)
    return lax.psum(local_scores, "layer")


def solution(mesh):
    return jax.shard_map(
        per_device,
        mesh=mesh,
        in_specs=(
            P("layer", ("groups", "ex"), None),
            P("layer", ("groups", "ex"), None),
            P("layer", None, None),
            P("layer", None, None),
            P(("groups", "ex"), None),
            P("groups"),
        ),
        out_specs=P("groups", "ex"),
        check_vma=False,
    )
```

profile of v0, /device:TPU:0, one launch (start us, length us, event | category | flops | bytes accessed | tf_op | source)
XLA Modules:
  0.0 555.9 jit_solution(8646806146413471716)
XLA Ops:
  6.5 0.8 copy.28
  8.2 1.5 fusion.1
  9.7 1.2 fusion.45
  11.3 5.0 fusion.108
  16.4 79.6 %reduce-scatter.2.cloned.1.call-done = f32[256,1024]{0,1:T(8,128)} async-done(((f32[1024,1024]{0,1:T(8,128)}), f32[256,1024]{0,1:T(8,128)}) %reduce-scatter.2.cloned.1.call-update) | async-done | bytes 1048592 | tf_op jit(solution)/shard_map/reduce_scatter | solution.py:28
  96.0 14.5 %all_gather.7 = f32[64,1024]{1,0:T(8,128)S(1)} all-gather(f32[16,1024]{1,0:T(8,128)S(1)} %fusion.97), channel_id=1, replica_groups=mesh['groups'=2,'ex'=4,'layer'=4] {'ex'}, dimensions={0}, use_global_device_ids=true | all-gather | bytes 327680 | tf_op jit(solution)/shard_map/all_gather | solution.py:22
  110.5 0.7 fusion.68
  111.1 67.8 %all-gather.2.cloned.1.call-done = f32[1024,1024]{0,1:T(8,128)} async-done(((f32[256,1024]{0,1:T(8,128)}), f32[1024,1024]{0,1:T(8,128)}) %all-gather.2.cloned.1.call-update) | async-done | bytes 4194320 | tf_op jit(solution)/shard_map/all_gather | solution.py:29
  178.9 2.9 select_reduce_fusion
  182.5 4.8 select_add_fusion
  187.3 5.5 copy.30
  192.8 4.5 fusion
  197.3 1.9 copy-done.3
  199.2 11.7 %cholesky.222 = f32[128,128]{1,0:T(8,128)S(1)} custom-call(f32[128,128]{1,0:T(8,128)S(1)} %cholesky.577), custom_call_target="Cholesky" | custom-call | tf_op jit(solution)/shard_map/jit(cholesky)/cholesky | solution.py:31
  211.0 9.8 %custom-call.66 = f32[1,128,128]{1,2,0:T(8,128)S(1)} custom-call(f32[1,128,128]{2,1,0:T(8,128)S(1)} %get-tuple-element.61), custom_call_target="InvertDiagBlocksLowerTriangular" | custom-call | tf_op jit(solution)/shard_map/jit(cholesky)/cholesky | solution.py:31
  220.8 1.5 fusion.25
  222.3 1.6 convolution_subtract_fusion
  223.9 0.8 copy-done.4
  224.7 11.7 %cholesky.243 = f32[128,128]{1,0:T(8,128)S(1)} custom-call(f32[128,128]{1,0:T(8,128)S(1)} %cholesky.581), custom_call_target="Cholesky" | custom-call | tf_op jit(solution)/shard_map/jit(cholesky)/cholesky | solution.py:31
  237.6 10.7 %custom-call.67 = f32[1,128,128]{1,2,0:T(8,128)S(1)} custom-call(f32[1,128,128]{2,1,0:T(8,128)} %get-tuple-element.59), custom_call_target="InvertDiagBlocksLowerTriangular" | custom-call | tf_op jit(solution)/shard_map/jit(cholesky)/cholesky | solution.py:31
  249.4 2.0 copy-done.1
  251.4 2.4 convolution_subtract_fusion.1
  253.8 11.7 %cholesky.466 = f32[128,128]{1,0:T(8,128)S(1)} custom-call(f32[128,128]{1,0:T(8,128)S(1)} %cholesky.586), custom_call_target="Cholesky" | custom-call | tf_op jit(solution)/shard_map/jit(cholesky)/cholesky | solution.py:31
  266.3 9.8 %custom-call.68 = f32[1,128,128]{1,2,0:T(8,128)S(1)} custom-call(f32[1,128,128]{2,1,0:T(8,128)S(1)} %get-tuple-element.57), custom_call_target="InvertDiagBlocksLowerTriangular" | custom-call | tf_op jit(solution)/shard_map/jit(cholesky)/cholesky | solution.py:31
  276.1 1.3 convolution_dynamic-update-slice_fusion.1
  277.4 3.5 convolution_subtract_fusion.2
  280.9 11.7 %cholesky.485 = f32[128,128]{1,0:T(8,128)S(1)} custom-call(f32[128,128]{1,0:T(8,128)S(1)} %cholesky.591), custom_call_target="Cholesky" | custom-call | tf_op jit(solution)/shard_map/jit(cholesky)/cholesky | solution.py:31
  293.4 9.8 %custom-call.69 = f32[1,128,128]{1,2,0:T(8,128)S(1)} custom-call(f32[1,128,128]{2,1,0:T(8,128)S(1)} %get-tuple-element.55), custom_call_target="InvertDiagBlocksLowerTriangular" | custom-call | tf_op jit(solution)/shard_map/jit(cholesky)/cholesky | solution.py:31
  303.2 1.1 convolution_dynamic-update-slice_fusion.2
  304.4 3.1 convolution_subtract_fusion.3
  307.5 11.8 %cholesky.504 = f32[128,128]{1,0:T(8,128)S(1)} custom-call(f32[128,128]{1,0:T(8,128)S(1)} %cholesky.596), custom_call_target="Cholesky" | custom-call | tf_op jit(solution)/shard_map/jit(cholesky)/cholesky | solution.py:31
  320.1 9.8 %custom-call.70 = f32[1,128,128]{1,2,0:T(8,128)S(1)} custom-call(f32[1,128,128]{2,1,0:T(8,128)S(1)} %get-tuple-element.53), custom_call_target="InvertDiagBlocksLowerTriangular" | custom-call | tf_op jit(solution)/shard_map/jit(cholesky)/cholesky | solution.py:31
  330.0 1.1 convolution_dynamic-update-slice_fusion.3
  331.1 3.1 convolution_subtract_fusion.4
  334.2 11.7 %cholesky.524 = f32[128,128]{1,0:T(8,128)S(1)} custom-call(f32[128,128]{1,0:T(8,128)S(1)} %cholesky.601), custom_call_target="Cholesky" | custom-call | tf_op jit(solution)/shard_map/jit(cholesky)/cholesky | solution.py:31
  346.6 9.8 %custom-call.71 = f32[1,128,128]{1,2,0:T(8,128)S(1)} custom-call(f32[1,128,128]{2,1,0:T(8,128)S(1)} %get-tuple-element.51), custom_call_target="InvertDiagBlocksLowerTriangular" | custom-call | tf_op jit(solution)/shard_map/jit(cholesky)/cholesky | solution.py:31
  356.5 1.0 convolution_dynamic-update-slice_fusion.5
  357.4 3.1 convolution_subtract_fusion.17
  360.5 11.7 %cholesky.544 = f32[128,128]{1,0:T(8,128)S(1)} custom-call(f32[128,128]{1,0:T(8,128)S(1)} %cholesky.606), custom_call_target="Cholesky" | custom-call | tf_op jit(solution)/shard_map/jit(cholesky)/cholesky | solution.py:31
  373.0 9.8 %custom-call.72 = f32[1,128,128]{1,2,0:T(8,128)S(1)} custom-call(f32[1,128,128]{2,1,0:T(8,128)S(1)} %get-tuple-element.49), custom_call_target="InvertDiagBlocksLowerTriangular" | custom-call | tf_op jit(solution)/shard_map/jit(cholesky)/cholesky | solution.py:31
  382.8 0.9 convolution_dynamic-update-slice_fusion.6
  383.8 2.1 convolution_subtract_fusion.20
  385.9 11.7 %cholesky.562 = f32[128,128]{1,0:T(8,128)S(1)} custom-call(f32[128,128]{1,0:T(8,128)S(1)} %convolution_subtract_fusion.20), custom_call_target="Cholesky" | custom-call | tf_op jit(solution)/shard_map/jit(cholesky)/cholesky | solution.py:31
  397.7 0.7 compare_reduce_fusion.5
  399.7 0.7 compare_reduce_fusion.2
  402.4 0.7 compare_reduce_fusion.6
  408.1 4.8 select_select_fusion
  412.9 28.5 %while.1 = (s32[]{:T(128)}, f32[1024,1024]{0,1:T(8,128)}, s32[8,2]{0,1:T(2,128)S(1)}, f32[8,128,128]{2,1,0:T(8,128)}, s32[]{:T(128)}) while((s32[]{:T(128)}, f32[1024,1024]{0,1:T(8,128)}, s32[8,2]{0,1:T(2,128)S(1)}, f32[8,128,128]{2,1,0:T(8,128)}, s32[]{:T(128)}) %tuple.50), condition=%wide.while_cond, body=%wide.while_body.sunk | while | flops 2 | bytes 393829 | solution.py:32
  413.5 2.2 dynamic-slice.7
  417.1 2.2 dynamic-slice.7
  420.7 2.2 dynamic-slice.7
  424.2 2.2 dynamic-slice.7
  427.8 2.2 dynamic-slice.7
  431.4 2.2 dynamic-slice.7
  434.9 2.2 dynamic-slice.7
  438.5 2.2 dynamic-slice.7
  441.4 79.5 %custom-call.73 = f32[8,128,128]{1,2,0:T(8,128)S(1)} custom-call(f32[8,128,128]{2,1,0:T(8,128)} %get-tuple-element.12), custom_call_target="InvertDiagBlocksLowerTriangular" | custom-call | tf_op jit(solution)/shard_map/jit(_cho_solve)/triangular_solve | solution.py:32
  521.3 1.3 convolution_subtract_fusion.16
  522.9 1.3 convolution_subtract_fusion.12
  524.5 1.4 convolution_subtract_fusion.11
  527.3 0.7 convolution_subtract_fusion.9
  528.3 0.9 convolution_subtract_fusion.15
  529.5 1.0 convolution_subtract_fusion.19
  537.0 11.8 %psum.7 = f32[256,16]{0,1:T(8,128)} all-reduce(f32[256,16]{0,1:T(8,128)S(1)} %fusion.109), channel_id=1, replica_groups=mesh['groups'=2,'ex'=4,'layer'=4] {'layer'}, use_global_device_ids=true, to_apply=%region_19.20 | all-reduce | flops 4096 | bytes 32768 | tf_op jit(solution)/shard_map/psum | solution.py:34
  (140 shorter events, 30.7 us)
Async XLA Ops:
  6.5 1.7 copy-start
  6.5 89.4 %reduce-scatter.2.cloned.1.call-start = ((), (), s32[]{:S(2)}) async-start(), calls=%async_computation.1 | async-start | bytes 5242880 | tf_op jit(solution)/shard_map/reduce_scatter | solution.py:28
  11.3 99.1 %copy-start.6 = (s32[256]{0:T(256)S(1)}, s32[256]{0:T(256)}, u32[]{:S(2)}) copy-start(s32[256]{0:T(256)} %param.11) | copy-start | bytes 3076
  16.4 162.6 %all-gather.2.cloned.1.call-start = ((), (), s32[]{:S(2)}) async-start(), calls=%async_computation.2 | async-start | bytes 5242880 | tf_op jit(solution)/shard_map/all_gather | solution.py:29
  197.3 1.9 copy-start.3
  223.9 0.8 copy-start.4
  237.5 11.4 %copy-start.5 = (f32[896,128]{1,0:T(8,128)S(1)}, f32[896,128]{1,0:T(8,128)}, u32[]{:S(2)}) copy-start(f32[896,128]{1,0:T(8,128)} %copy-done.4) | copy-start | bytes 1376260
  249.4 2.0 copy-start.1
  520.9 5.4 copy-start.2
Sparse Core Ops, SparseCore 0:
  16.5 79.4 reduce-scatter.1
  97.6 81.2 all-gather.1
where the time goes:
time: 560 us; the launch traced here: 556 us
  other arithmetic  266 us (48%)
  waiting for transfers between devices  147 us (26%)
  matrix products  50.4 us (9%)
  local copies, waits for them, and re-layouts  45.2 us (8%)
  blocking collectives  26.2 us (5%)
  between operations  20 us (4%)
    another operation x30, other arithmetic, per_device(): jnp.linalg.cholesky(gram_matrix + damping * jnp.eye(width, dtype=jnp.floa...  169 us
    another operation x3, other arithmetic, per_device(): precond = jax.scipy.linalg.cho_solve((factor, True), queries.T).T  84.4 us
    reduce_scatter x1, waiting for transfers between devices, per_device(): lax.psum_scatter(partial_gram, 'ex', scatter_dimension=0, tiled=True)  79.6 us
    all_gather x1, waiting for transfers between devices, per_device(): gram_matrix = lax.all_gather(gram_rows, 'ex', axis=0, tiled=True)  67.8 us
    another operation x41, local copies, waits for them, and re-layouts  29.2 us
    another operation x14, matrix products, per_device(): jnp.linalg.cholesky(gram_matrix + damping * jnp.eye(width, dtype=jnp.floa...  26.3 us
    another operation x30, matrix products, per_device(): precond = jax.scipy.linalg.cho_solve((factor, True), queries.T).T  14.8 us
    all_gather x1, blocking collectives, per_device(): all_features = lax.all_gather(features, 'ex', axis=0, tiled=True)  14.5 us
  transfers between devices with their start and end apart: 2, of which 2 were waited for; matrix products, arithmetic and copies ran while one was open for 0% of the time, Pallas kernels for 0%

commit v1 on v0

v1 whole, which is shorter than its diff:
```python
import functools

import jax
import jax.numpy as jnp
from jax import lax
from jax.experimental import pallas as pl
from jax.experimental.pallas import tpu as pltpu
from jax.sharding import PartitionSpec as P

F32 = jnp.float32
BF16 = jnp.bfloat16
CHUNKS = 4


def nt(a, b):
    return lax.dot_general(a, b, (((1,), (1,)), ((), ())), preferred_element_type=F32)


def nn(a, b):
    return lax.dot_general(a, b, (((1,), (0,)), ((), ())), preferred_element_type=F32)


def tn(a, b):
    return lax.dot_general(a, b, (((0,), (0,)), ((), ())), preferred_element_type=F32)


def split3(x):
    hi = x.astype(BF16)
    rest = x - hi.astype(F32)
    mid = rest.astype(BF16)
    low = (rest - mid.astype(F32)).astype(BF16)
    return hi, mid, low


def split2(x):
    hi = x.astype(BF16)
    return hi, (x - hi.astype(F32)).astype(BF16)


def mm(a, b):
    ah, al = split2(a)
    bh, bl = split2(b)
    return nn(ah, bh) + (nn(ah, bl) + nn(al, bh))


def exact_nn(a, b):
    return lax.dot_general(a, b, (((1,), (0,)), ((), ())), precision=lax.Precision.HIGHEST, preferred_element_type=F32)


def project_kernel(lens_hbm, li_ref, og_ref, pi_ref, po_ref, out_ref, lens_ref, li_v, og_v, pi_v, po_v, sems):
    ff = og_ref.shape[2]
    step = ff // CHUNKS
    copies = [
        pltpu.make_async_copy(pi_ref.at[0], pi_v, sems.at[0]),
        pltpu.make_async_copy(li_ref.at[0], li_v, sems.at[1]),
        pltpu.make_async_copy(po_ref.at[0], po_v, sems.at[2]),
        pltpu.make_async_copy(lens_hbm, lens_ref, sems.at[3]),
    ]
    for c in range(CHUNKS):
        cols = pl.ds(c * step, step)
        copies.append(pltpu.make_async_copy(og_ref.at[0, :, cols], og_v.at[:, cols], sems.at[4 + c]))
    for copy in copies:
        copy.start()
    rank = pi_ref.shape[1]
    frames = li_ref.shape[1]
    positions = lax.broadcasted_iota(jnp.int32, (8, frames), 1)
    copies[3].wait()
    ids = jnp.zeros((8, frames), F32)
    end = lens_ref[0, 0]
    for j in range(1, lens_ref.shape[1]):
        ids = ids + jnp.where(positions >= end, 1.0, 0.0)
        end = end + lens_ref[0, j]
    out_ref[2 * rank:, :] = ids
    copies[0].wait()
    copies[1].wait()
    out_ref[rank:2 * rank, :] = nt(pi_v[...], li_v[...])
    copies[2].wait()
    total = jnp.zeros((rank, frames), F32)
    for c in range(CHUNKS):
        copies[4 + c].wait()
        total = total + nt(po_v[:, c * step:(c + 1) * step], og_v[:, c * step:(c + 1) * step])
    out_ref[:rank, :] = total


def solve_kernel(width, per_dev, rank, *refs):
    packets, out_ref, s_ref = refs[:-2], refs[-2], refs[-1]
    frames = packets[0].shape[1]
    count = len(packets)
    total = count * per_dev

    def terms(lo):
        x = jnp.concatenate([p[lo:lo + rank, :] for p in packets], axis=1)
        hi, mid, low = split3(x)
        return (
            jnp.concatenate([hi, hi, mid, hi, low, mid], axis=0),
            jnp.concatenate([hi, mid, hi, low, hi, mid], axis=0),
        )

    left_o, right_o = terms(0)
    left_i, right_i = terms(rank)
    row = lax.broadcasted_iota(jnp.int32, (total, frames), 0).astype(F32)
    member = jnp.concatenate(
        [jnp.where(p[2 * rank:2 * rank + 1, :] + float(k * per_dev) == row, 1.0, 0.0) for k, p in enumerate(packets)], axis=1
    ).astype(BF16)
    kernel = jnp.zeros((total, total), F32)
    for k in range(count):
        cols = slice(k * frames, (k + 1) * frames)
        block = tn(left_o[:, cols], right_o) * tn(left_i[:, cols], right_i)
        hi, mid, low = split3(block)
        part = (nt(low, member) + nt(mid, member)) + nt(hi, member)
        hi, mid, low = split3(part)
        m = member[:, cols]
        kernel = kernel + ((nn(m, low) + nn(m, mid)) + nn(m, hi))

    ids0 = lax.broadcasted_iota(jnp.int32, (total, total), 0)
    ids1 = lax.broadcasted_iota(jnp.int32, (total, total), 1)
    diagonal = ids0 == ids1
    eye = jnp.where(diagonal, 1.0, 0.0)
    damp = jnp.sum(jnp.where(diagonal, kernel, 0.0), keepdims=True) * (0.1 / width)
    scale = jnp.sum(jnp.where(diagonal, kernel, 0.0), axis=0, keepdims=True) + damp
    ratio = damp / scale
    column = jnp.sum(jnp.where(diagonal, ratio, 0.0), axis=1, keepdims=True)
    e1 = jnp.where(diagonal, 0.0, -kernel / scale)
    mine = e1[:per_dev] + eye[:per_dev]
    e2 = mm(e1, e1)
    mine = mine + mm(mine, e2)
    e4 = mm(e2, e2)
    mine = mine + mm(mine, e4)
    e8 = mm(e4, e4)
    mine = mine + mm(mine, e8)
    squares = e8 * e8
    left = jnp.sum(squares * column)
    spread = jnp.sum(squares * column * (scale / damp))
    good = (left <= 1e-5) & (spread <= 0.02)
    s_ref[...] = eye[:per_dev] - column[:per_dev] * mine

    @pl.when(jnp.logical_not(good))
    def _():
        full = kernel + damp * eye

        def sweep(k, a):
            r = jnp.sum(jnp.where(ids0 == k, a, 0.0), axis=0, keepdims=True)
            c = jnp.sum(jnp.where(ids1 == k, a, 0.0), axis=1, keepdims=True)
            p = 1.0 / jnp.sum(jnp.where(ids1[:1] == k, r, 0.0), axis=1, keepdims=True)
            inner = a - c * (r * p)
            edge = jnp.where(ids0 == k, r * p, c * p)
            swept = jnp.where((ids0 == k) | (ids1 == k), edge, inner)
            return jnp.where((ids0 == k) & (ids1 == k), -p, swept)

        inverse = -lax.fori_loop(0, total, sweep, full)
        inverse = inverse + exact_nn(inverse, eye - exact_nn(full, inverse))
        s_ref[...] = eye[:per_dev] - damp * inverse[:per_dev]

    out_ref[...] = s_ref[...]


def score_kernel(ex_count, per_dev, a_ref, b_ref, c_ref, d_ref, q_ref, out_ref):
    summed = (a_ref[...] + b_ref[...]) + (c_ref[...] + d_ref[...])
    total = summed.shape[1]
    z = lax.axis_index("ex")
    q = q_ref[...]
    place = jnp.bitwise_xor(q // per_dev, z) * per_dev + q % per_dev
    rows = lax.broadcasted_iota(jnp.int32, (total, q.shape[1]), 0)
    chosen = jnp.where(rows == place, 1.0, 0.0).astype(BF16)
    hi, mid, low = split3(summed)
    out_ref[...] = (nn(low, chosen) + nn(mid, chosen)) + nn(hi, chosen)


def vmem():
    return pl.BlockSpec(memory_space=pltpu.VMEM)


def swap(x, axis, count, k):
    return lax.ppermute(x, axis, [(i, i ^ k) for i in range(count)])


def small_device(ex_count, layer_count, layer_inputs, out_grads, proj_in, proj_out, frame_lengths, query_ids):
    frames = layer_inputs.shape[1]
    rank = proj_in.shape[2]
    per_dev = frame_lengths.shape[1]
    total = ex_count * per_dev
    hbm = pl.BlockSpec(memory_space=pltpu.HBM)
    packet = pl.pallas_call(
        project_kernel,
        out_shape=jax.ShapeDtypeStruct((2 * rank + 8, frames), F32),
        in_specs=[hbm] * 5,
        out_specs=vmem(),
        scratch_shapes=[
            pltpu.SMEM(frame_lengths.shape, jnp.int32),
            pltpu.VMEM(layer_inputs.shape[1:], BF16),
            pltpu.VMEM(out_grads.shape[1:], BF16),
            pltpu.VMEM((rank, proj_in.shape[1]), BF16),
            pltpu.VMEM((rank, proj_out.shape[1]), BF16),
            pltpu.SemaphoreType.DMA((4 + CHUNKS,)),
        ],
        compiler_params=pltpu.CompilerParams(vmem_limit_bytes=56508416),
        name="project",
    )(frame_lengths, layer_inputs, out_grads, jnp.swapaxes(proj_in, 1, 2), jnp.swapaxes(proj_out, 1, 2))
    packets = [packet] + [swap(packet, "ex", ex_count, k) for k in range(1, ex_count)]
    share = pl.pallas_call(
        functools.partial(solve_kernel, rank * rank, per_dev, rank),
        out_shape=jax.ShapeDtypeStruct((per_dev, total), F32),
        in_specs=[vmem()] * ex_count,
        out_specs=vmem(),
        scratch_shapes=[pltpu.VMEM((per_dev, total), F32)],
        compiler_params=pltpu.CompilerParams(vmem_limit_bytes=16 * 1024 * 1024),
        name="solve",
    )(*packets)
    shares = [share] + [swap(share, "layer", layer_count, k) for k in range(1, layer_count)]
    scores = pl.pallas_call(
        functools.partial(score_kernel, ex_count, per_dev),
        out_shape=jax.ShapeDtypeStruct((per_dev, query_ids.shape[0]), F32),
        in_specs=[vmem()] * 5,
        out_specs=vmem(),
        compiler_params=pltpu.CompilerParams(vmem_limit_bytes=16 * 1024 * 1024),
        name="score",
    )(*shares, query_ids.reshape(1, -1))
    return scores.T


def large_device(layer_inputs, out_grads, proj_in, proj_out, frame_lengths, query_ids):
    frame_count = layer_inputs.shape[1]
    in_proj = jnp.dot(layer_inputs[0], proj_in[0], preferred_element_type=F32)
    out_proj = jnp.dot(out_grads[0], proj_out[0], preferred_element_type=F32)
    rank = in_proj.shape[1]
    width = rank * rank
    outer_terms = (out_proj[:, :, None] * in_proj[:, None, :]).reshape(frame_count, width)
    lengths = frame_lengths[0]
    end_frames = jnp.cumsum(lengths)
    starts = end_frames - lengths
    positions = jnp.arange(frame_count, dtype=jnp.int32)
    member = ((positions[None, :] >= starts[:, None]) & (positions[None, :] < end_frames[:, None])).astype(F32)
    features = jnp.dot(member, outer_terms, precision=lax.Precision.HIGHEST)
    all_features = lax.all_gather(features, "ex", axis=0, tiled=True)
    count = all_features.shape[0]
    kernel = lax.dot_general(
        all_features, all_features, (((1,), (1,)), ((), ())), precision=lax.Precision.HIGHEST, preferred_element_type=F32
    )
    damping = 0.1 * jnp.trace(kernel) / width
    factor = jnp.linalg.cholesky(kernel + damping * jnp.eye(count, dtype=F32))
    mine = lax.axis_index("ex") * lengths.shape[0] + jnp.arange(lengths.shape[0])
    picked = (jnp.arange(count)[:, None] == mine[None, :]).astype(F32)
    share = picked - damping * jax.scipy.linalg.cho_solve((factor, True), picked)
    summed = lax.psum(share, "layer")
    chosen = (query_ids[:, None] == jnp.arange(count, dtype=jnp.int32)[None, :]).astype(F32)
    return jnp.dot(chosen, summed, precision=lax.Precision.HIGHEST)


def solution(mesh):
    ex_count, layer_count = mesh.shape["ex"], mesh.shape["layer"]
    if ex_count == 4 and layer_count == 4:
        per_device = functools.partial(small_device, ex_count, layer_count)
    else:
        per_device = large_device
    return jax.shard_map(
        per_device,
        mesh=mesh,
        in_specs=(
            P("layer", ("groups", "ex"), None),
            P("layer", ("groups", "ex"), None),
            P("layer", None, None),
            P("layer", None, None),
            P(("groups", "ex"), None),
            P("groups"),
        ),
        out_specs=P("groups", "ex"),
        check_vma=False,
    )
```

time: 560 us -> 27.5 us (0.05)
  other arithmetic: 266 us -> 0 us
  waiting for transfers between devices: 147 us -> 6.09 us
  matrix products: 50.4 us -> 0 us
  local copies, waits for them, and re-layouts: 45.2 us -> 0.67 us
  blocking collectives: 26.2 us -> 0 us
  between operations: 20 us -> 0.03 us
  Pallas kernels: 0 us -> 12.9 us
  starting transfers between devices: 0.04 us -> 7.68 us
    another operation x35 -> x0, other arithmetic: 253 us -> none  [the longest x30 169 us: per_device(): jnp.linalg.cholesky(gram_matrix + damping * jnp.eye(width, dtype=jnp.floa...]
    reduce_scatter x1 -> x0, waiting for transfers between devices: 79.6 us -> none  [per_device(): lax.psum_scatter(partial_gram, 'ex', scatter_dimension=0, tiled=True)]
    all_gather x1 -> x0, waiting for transfers between devices: 67.8 us -> none  [per_device(): gram_matrix = lax.all_gather(gram_rows, 'ex', axis=0, tiled=True)]
    another operation x44 -> x0, matrix products: 41.1 us -> none  [the longest x14 26.3 us: per_device(): jnp.linalg.cholesky(gram_matrix + damping * jnp.eye(width, dtype=jnp.floa...]
    another operation x71 -> x0, local copies, waits for them, and re-layouts: 34.9 us -> none
    all_gather x1 -> x0, blocking collectives: 14.5 us -> none  [per_device(): all_features = lax.all_gather(features, 'ex', axis=0, tiled=True)]
    pallas_call x0 -> x3, Pallas kernels: none -> 12.9 us  [the longest x1 9.95 us: small_device(): pl.pallas_call(functools.partial(solve_kernel, rank * rank, per_dev, rank...]
    psum x1 -> x0, blocking collectives: 11.8 us -> none  [per_device(): return lax.psum(local_scores, 'layer')]
  transfers between devices with their start and end apart: 2 -> 6, of which waited for: 2 -> 4; matrix products, arithmetic and copies ran while one was open for 0% -> 0% of each run, Pallas kernels for 0% -> 0%
where the time goes in v1:
time: 27.5 us; the launch traced here: 27.4 us
  Pallas kernels  12.9 us (47%)
  starting transfers between devices  7.68 us (28%)
  waiting for transfers between devices  6.09 us (22%)
  local copies, waits for them, and re-layouts  0.67 us (2%)
    pallas_call x1, Pallas kernels, small_device(): pl.pallas_call(functools.partial(solve_kernel, rank * rank, per_dev, rank...  9.95 us
    ppermute x6, starting transfers between devices, swap(): return lax.ppermute(x, axis, [(i, i ^ k) for i in range(count)])  7.68 us
    ppermute x6, waiting for transfers between devices, swap(): return lax.ppermute(x, axis, [(i, i ^ k) for i in range(count)])  6.09 us
    pallas_call x1, Pallas kernels, small_device(): pl.pallas_call(project_kernel, out_shape=jax.ShapeDtypeStruct((2 * rank +...  2.22 us
    pallas_call x1, Pallas kernels, small_device(): pl.pallas_call(functools.partial(score_kernel, ex_count, per_dev), out_sh...  0.76 us
    unnamed x4, local copies, waits for them, and re-layouts  0.67 us
  transfers between devices with their start and end apart: 6, of which 4 were waited for; matrix products, arithmetic and copies ran while one was open for 0% of the time, Pallas kernels for 0%

profile of v1, /device:TPU:0, one launch (start us, length us, event | category | flops | bytes accessed | tf_op | source)
XLA Modules:
  0.0 27.4 jit_solution(8873513225197664973)
XLA Ops:
  0.0 0.0 copy-start
  0.0 0.0 copy-start.1
  0.0 0.7 %copy-done.1 = s32[1,16]{1,0:T(1,128)S(1)} copy-done((s32[1,16]{1,0:T(1,128)S(1)}, s32[1,16]{1,0:T(1,128)}, u32[]{:S(2)}) %copy-start.1) | copy-done | bytes 88
  0.7 2.2 %project.1.refs_0_ = f32[72,128]{1,0:T(8,128)S(1)} custom-call(s32[1,16]{1,0:T(1,128)S(1)} %copy-done.1, bf16[1,128,1280]{2,1,0:T(8,128)(2,1)} %li_ref.1, bf16[1,128,5120]{2,1,0:T(8,128)(2,1)} %og_ref.1, bf16[1,32,1280]{2,1,0:T(8,128)(2,1)} %bitcast.6, bf16[1,32,5120]{2,1,0:T(8,128)(2,1)} %bitcast.5), custom_call_target="tpu_custom_call" | custom-call | tf_op jit(solution)/shard_map/project/pallas_call | solution.py:183
  2.9 5.1 %collective-permute-start.2 = (f32[72,128]{1,0:T(8,128)S(1)}, f32[72,128]{1,0:T(8,128)S(1)}, u32[]{:S(2)}, u32[]{:S(2)}) collective-permute-start(f32[72,128]{1,0:T(8,128)S(1)} %project.1.refs_0_), channel_id=1, source_target_pairs={{0,12},{4,8},{8,4},{12,0},{1,13},{5,9},{9,5},{13,1},{2,14},{6,10},... | collective-permute-start | bytes 110600 | tf_op jit(solution)/shard_map/ppermute | solution.py:174
  8.0 0.0 collective-permute-start.1
  8.0 0.6 %collective-permute-start = (f32[72,128]{1,0:T(8,128)S(1)}, f32[72,128]{1,0:T(8,128)S(1)}, u32[]{:S(2)}, u32[]{:S(2)}) collective-permute-start(f32[72,128]{1,0:T(8,128)S(1)} %project.1.refs_0_), channel_id=1, source_target_pairs={{0,4},{4,0},{8,12},{12,8},{1,5},{5,1},{9,13},{13,9},{2,6},{6,2},{1... | collective-permute-start | bytes 110600 | tf_op jit(solution)/shard_map/ppermute | solution.py:174
  8.7 1.3 %collective-permute-done.2.refs_3_ = f32[72,128]{1,0:T(8,128)S(1)} collective-permute-done((f32[72,128]{1,0:T(8,128)S(1)}, f32[72,128]{1,0:T(8,128)S(1)}, u32[]{:S(2)}, u32[]{:S(2)}) %collective-permute-start.2) | collective-permute-done | bytes 36896 | tf_op jit(solution)/shard_map/ppermute | solution.py:174
  10.0 2.9 %collective-permute-done.1.refs_2_ = f32[72,128]{1,0:T(8,128)S(1)} collective-permute-done((f32[72,128]{1,0:T(8,128)S(1)}, f32[72,128]{1,0:T(8,128)S(1)}, u32[]{:S(2)}, u32[]{:S(2)}) %collective-permute-start.1) | collective-permute-done | bytes 36896 | tf_op jit(solution)/shard_map/ppermute | solution.py:174
  12.9 0.0 collective-permute-done.refs_1_
  12.9 9.9 %solve.1.a_ref = f32[16,64]{1,0:T(8,128)S(1)} custom-call(f32[72,128]{1,0:T(8,128)S(1)} %project.1.refs_0_, f32[72,128]{1,0:T(8,128)S(1)} %collective-permute-done.refs_1_, f32[72,128]{1,0:T(8,128)S(1)} %collective-permute-done.1.refs_2_, f32[72,128]{1,0:T(8,128)S(1)} %collective-permute-done.2.refs_3_), custom_call_target="tpu_custom_call" | custom-call | tf_op jit(solution)/shard_map/solve/pallas_call | solution.py:200
  22.8 0.1 collective-permute-start.5
  22.9 1.6 %collective-permute-start.4 = (f32[16,64]{1,0:T(8,128)S(1)}, f32[16,64]{1,0:T(8,128)S(1)}, u32[]{:S(2)}, u32[]{:S(2)}) collective-permute-start(f32[16,64]{1,0:T(8,128)S(1)} %solve.1.a_ref), channel_id=1, source_target_pairs={{0,2},{1,3},{2,0},{3,1},{4,6},{5,7},{6,4},{7,5},{8,10},{9,11},{10,... | collective-permute-start | bytes 12296 | tf_op jit(solution)/shard_map/ppermute | solution.py:174
  24.5 0.3 %collective-permute-start.3 = (f32[16,64]{1,0:T(8,128)S(1)}, f32[16,64]{1,0:T(8,128)S(1)}, u32[]{:S(2)}, u32[]{:S(2)}) collective-permute-start(f32[16,64]{1,0:T(8,128)S(1)} %solve.1.a_ref), channel_id=1, source_target_pairs={{0,1},{1,0},{2,3},{3,2},{4,5},{5,4},{6,7},{7,6},{8,9},{9,8},{10,11... | collective-permute-start | bytes 12296 | tf_op jit(solution)/shard_map/ppermute | solution.py:174
  24.8 1.2 %collective-permute-done.5.d_ref = f32[16,64]{1,0:T(8,128)S(1)} collective-permute-done((f32[16,64]{1,0:T(8,128)S(1)}, f32[16,64]{1,0:T(8,128)S(1)}, u32[]{:S(2)}, u32[]{:S(2)}) %collective-permute-start.5) | collective-permute-done | bytes 4128 | tf_op jit(solution)/shard_map/ppermute | solution.py:174
  26.0 0.6 %collective-permute-done.4.c_ref = f32[16,64]{1,0:T(8,128)S(1)} collective-permute-done((f32[16,64]{1,0:T(8,128)S(1)}, f32[16,64]{1,0:T(8,128)S(1)}, u32[]{:S(2)}, u32[]{:S(2)}) %collective-permute-start.4) | collective-permute-done | bytes 4128 | tf_op jit(solution)/shard_map/ppermute | solution.py:174
  26.6 0.0 collective-permute-done.3.b_ref
  26.6 0.0 copy-done
  26.6 0.8 %score.1 = f32[16,256]{1,0:T(8,128)} custom-call(f32[16,64]{1,0:T(8,128)S(1)} %solve.1.a_ref, f32[16,64]{1,0:T(8,128)S(1)} %collective-permute-done.3.b_ref, f32[16,64]{1,0:T(8,128)S(1)} %collective-permute-done.4.c_ref, f32[16,64]{1,0:T(8,128)S(1)} %collective-permute-done.5.d_ref, s32[1,256]{1,0:T(1,128)S(1)} %bitcast.4), custom_call_target="tpu_custom_call" | custom-call | tf_op jit(solution)/shard_map/score/pallas_call | solution.py:210
Async XLA Ops:
  0.0 26.6 %copy-start = (s32[256]{0:T(256)S(1)}, s32[256]{0:T(256)}, u32[]{:S(2)}) copy-start(s32[256]{0:T(256)} %param.11) | copy-start | bytes 3076
  0.0 0.7 %copy-start.1 = (s32[1,16]{1,0:T(1,128)S(1)}, s32[1,16]{1,0:T(1,128)}, u32[]{:S(2)}) copy-start(s32[1,16]{1,0:T(1,128)} %lens_hbm.1) | copy-start | bytes 196
  2.9 7.1 %collective-permute-start.2 = (f32[72,128]{1,0:T(8,128)S(1)}, f32[72,128]{1,0:T(8,128)S(1)}, u32[]{:S(2)}, u32[]{:S(2)}) collective-permute-start(f32[72,128]{1,0:T(8,128)S(1)} %project.1.refs_0_), channel_id=1, source_target_pairs={{0,12},{4,8},{8,4},{12,0},{1,13},{5,9},{9,5},{13,1},{2,14},{6,10},... | collective-permute-start | bytes 110600 | tf_op jit(solution)/shard_map/ppermute | solution.py:174
  8.0 4.9 %collective-permute-start.1 = (f32[72,128]{1,0:T(8,128)S(1)}, f32[72,128]{1,0:T(8,128)S(1)}, u32[]{:S(2)}, u32[]{:S(2)}) collective-permute-start(f32[72,128]{1,0:T(8,128)S(1)} %project.1.refs_0_), channel_id=1, source_target_pairs={{0,8},{4,12},{8,0},{12,4},{1,9},{5,13},{9,1},{13,5},{2,10},{6,14},... | collective-permute-start | bytes 110600 | tf_op jit(solution)/shard_map/ppermute | solution.py:174
  8.0 4.9 %collective-permute-start = (f32[72,128]{1,0:T(8,128)S(1)}, f32[72,128]{1,0:T(8,128)S(1)}, u32[]{:S(2)}, u32[]{:S(2)}) collective-permute-start(f32[72,128]{1,0:T(8,128)S(1)} %project.1.refs_0_), channel_id=1, source_target_pairs={{0,4},{4,0},{8,12},{12,8},{1,5},{5,1},{9,13},{13,9},{2,6},{6,2},{1... | collective-permute-start | bytes 110600 | tf_op jit(solution)/shard_map/ppermute | solution.py:174
  22.8 3.2 %collective-permute-start.5 = (f32[16,64]{1,0:T(8,128)S(1)}, f32[16,64]{1,0:T(8,128)S(1)}, u32[]{:S(2)}, u32[]{:S(2)}) collective-permute-start(f32[16,64]{1,0:T(8,128)S(1)} %solve.1.a_ref), channel_id=1, source_target_pairs={{0,3},{1,2},{2,1},{3,0},{4,7},{5,6},{6,5},{7,4},{8,11},{9,10},{10,... | collective-permute-start | bytes 12296 | tf_op jit(solution)/shard_map/ppermute | solution.py:174
  22.9 3.7 %collective-permute-start.4 = (f32[16,64]{1,0:T(8,128)S(1)}, f32[16,64]{1,0:T(8,128)S(1)}, u32[]{:S(2)}, u32[]{:S(2)}) collective-permute-start(f32[16,64]{1,0:T(8,128)S(1)} %solve.1.a_ref), channel_id=1, source_target_pairs={{0,2},{1,3},{2,0},{3,1},{4,6},{5,7},{6,4},{7,5},{8,10},{9,11},{10,... | collective-permute-start | bytes 12296 | tf_op jit(solution)/shard_map/ppermute | solution.py:174
  24.5 2.2 %collective-permute-start.3 = (f32[16,64]{1,0:T(8,128)S(1)}, f32[16,64]{1,0:T(8,128)S(1)}, u32[]{:S(2)}, u32[]{:S(2)}) collective-permute-start(f32[16,64]{1,0:T(8,128)S(1)} %solve.1.a_ref), channel_id=1, source_target_pairs={{0,1},{1,0},{2,3},{3,2},{4,5},{5,4},{6,7},{7,6},{8,9},{9,8},{10,11... | collective-permute-start | bytes 12296 | tf_op jit(solution)/shard_map/ppermute | solution.py:174

commit v2 on v1

--- a/solution.py
+++ b/solution.py
@@ -10,6 +10,8 @@
 F32 = jnp.float32
 BF16 = jnp.bfloat16
 CHUNKS = 4
+RING = (0, 2, 1, 3)
+HOPS = (0, 2, 3, 1)
 
 
 def nt(a, b):
@@ -43,8 +45,8 @@
     return nn(ah, bh) + (nn(ah, bl) + nn(al, bh))
 
 
-def exact_nn(a, b):
-    return lax.dot_general(a, b, (((1,), (0,)), ((), ())), precision=lax.Precision.HIGHEST, preferred_element_type=F32)
+def exact(a, b, dims):
+    return lax.dot_general(a, b, (dims, ((), ())), precision=lax.Precision.HIGHEST, preferred_element_type=F32)
 
 
 def project_kernel(lens_hbm, li_ref, og_ref, pi_ref, po_ref, out_ref, lens_ref, li_v, og_v, pi_v, po_v, sems):
@@ -82,35 +84,65 @@
     out_ref[:rank, :] = total
 
 
+def orthogonal_shares(width, per_dev, rank, packets, member, v_ref):
+    total = member.shape[0]
+    blocks, lanes = v_ref.shape[0] - 1, v_ref.shape[2]
+    per = lanes // rank
+    in_proj = jnp.concatenate([jnp.concatenate([p[rank:2 * rank, :] for p in packets], axis=1)] * per, axis=0)
+    owner = lax.broadcasted_iota(jnp.int32, in_proj.shape, 0) // rank
+
+    def fill(g, carry):
+        block = jnp.zeros((total, lanes), F32)
+        for s in range(per):
+            out_row = jnp.concatenate([p[pl.ds(g * per + s, 1), :] for p in packets], axis=1)
+            block = block + exact(member * out_row, jnp.where(owner == s, in_proj, 0.0), ((1,), (1,)))
+        v_ref[pl.ds(g, 1)] = block[None]
+        return carry
+
+    lax.fori_loop(0, blocks, fill, 0)
+    features = v_ref[:blocks]
+    damp = jnp.sum(features * features, keepdims=True)[0] * (0.1 / width)
+    row = lax.broadcasted_iota(jnp.int32, (total, lanes), 0)
+    lane = lax.broadcasted_iota(jnp.int32, (total, lanes), 1)
+    v_ref[blocks] = jnp.where(row == lane, jnp.sqrt(damp), 0.0)
+
+    def step(k, carry):
+        v = v_ref[...]
+        rows = lax.broadcasted_iota(jnp.int32, v.shape, 1)
+        q = jnp.sum(jnp.where(rows == k, v, 0.0), axis=1, keepdims=True)
+        size = jnp.sum(jnp.sum(q * q, axis=0, keepdims=True), axis=2, keepdims=True)
+        q = q / jnp.sqrt(size)
+        along = jnp.sum(jnp.sum(v * q, axis=0, keepdims=True), axis=2, keepdims=True)
+        v_ref[...] = jnp.where(rows > k, v - along * q, jnp.where(rows == k, q, v))
+        return carry
+
+    lax.fori_loop(0, total, step, 0)
+    last = v_ref[blocks]
+    inverse = exact(last, last, ((0,), (0,)))
+    return jnp.where(row == lane, 1.0, 0.0)[:per_dev, :total] - inverse[:per_dev, :total]
+
+
 def solve_kernel(width, per_dev, rank, *refs):
-    packets, out_ref, s_ref = refs[:-2], refs[-2], refs[-1]
+    packets, out_ref, s_ref, v_ref = refs[:-3], refs[-3], refs[-2], refs[-1]
     frames = packets[0].shape[1]
     count = len(packets)
     total = count * per_dev
 
     def terms(lo):
         x = jnp.concatenate([p[lo:lo + rank, :] for p in packets], axis=1)
-        hi, mid, low = split3(x)
-        return (
-            jnp.concatenate([hi, hi, mid, hi, low, mid], axis=0),
-            jnp.concatenate([hi, mid, hi, low, hi, mid], axis=0),
-        )
+        hi, low = split2(x)
+        return jnp.concatenate([hi, hi, low], axis=0), jnp.concatenate([hi, low, hi], axis=0)
 
     left_o, right_o = terms(0)
     left_i, right_i = terms(rank)
     row = lax.broadcasted_iota(jnp.int32, (total, frames), 0).astype(F32)
-    member = jnp.concatenate(
+    membership = jnp.concatenate(
         [jnp.where(p[2 * rank:2 * rank + 1, :] + float(k * per_dev) == row, 1.0, 0.0) for k, p in enumerate(packets)], axis=1
-    ).astype(BF16)
-    kernel = jnp.zeros((total, total), F32)
-    for k in range(count):
-        cols = slice(k * frames, (k + 1) * frames)
-        block = tn(left_o[:, cols], right_o) * tn(left_i[:, cols], right_i)
-        hi, mid, low = split3(block)
-        part = (nt(low, member) + nt(mid, member)) + nt(hi, member)
-        hi, mid, low = split3(part)
-        m = member[:, cols]
-        kernel = kernel + ((nn(m, low) + nn(m, mid)) + nn(m, hi))
+    )
+    member = membership.astype(BF16)
+    hi, low = split2(tn(left_o, right_o) * tn(left_i, right_i))
+    hi, low = split2(nt(low, member) + nt(hi, member))
+    kernel = nn(member, low) + nn(member, hi)
 
     ids0 = lax.broadcasted_iota(jnp.int32, (total, total), 0)
     ids1 = lax.broadcasted_iota(jnp.int32, (total, total), 1)
@@ -131,35 +163,31 @@
     squares = e8 * e8
     left = jnp.sum(squares * column)
     spread = jnp.sum(squares * column * (scale / damp))
-    good = (left <= 1e-5) & (spread <= 0.02)
+    good = (left <= 1e-5) & (spread <= 0.005)
     s_ref[...] = eye[:per_dev] - column[:per_dev] * mine
 
     @pl.when(jnp.logical_not(good))
     def _():
-        full = kernel + damp * eye
-
-        def sweep(k, a):
-            r = jnp.sum(jnp.where(ids0 == k, a, 0.0), axis=0, keepdims=True)
-            c = jnp.sum(jnp.where(ids1 == k, a, 0.0), axis=1, keepdims=True)
-            p = 1.0 / jnp.sum(jnp.where(ids1[:1] == k, r, 0.0), axis=1, keepdims=True)
-            inner = a - c * (r * p)
-            edge = jnp.where(ids0 == k, r * p, c * p)
-            swept = jnp.where((ids0 == k) | (ids1 == k), edge, inner)
-            return jnp.where((ids0 == k) & (ids1 == k), -p, swept)
-
-        inverse = -lax.fori_loop(0, total, sweep, full)
-        inverse = inverse + exact_nn(inverse, eye - exact_nn(full, inverse))
-        s_ref[...] = eye[:per_dev] - damp * inverse[:per_dev]
+        e16 = mm(e8, e8)
+        s_ref[...] = eye[:per_dev] - column[:per_dev] * (mine + mm(mine, e16))
+        near = (jnp.sum(e16 * e16 * column) <= 1e-5) & (spread <= 0.05)
+
+        @pl.when(jnp.logical_not(near))
+        def _():
+            s_ref[...] = orthogonal_shares(width, per_dev, rank, packets, membership, v_ref)
 
     out_ref[...] = s_ref[...]
 
 
-def score_kernel(ex_count, per_dev, a_ref, b_ref, c_ref, d_ref, q_ref, out_ref):
+def score_kernel(per_dev, a_ref, b_ref, c_ref, d_ref, q_ref, out_ref):
     summed = (a_ref[...] + b_ref[...]) + (c_ref[...] + d_ref[...])
     total = summed.shape[1]
-    z = lax.axis_index("ex")
     q = q_ref[...]
-    place = jnp.bitwise_xor(q // per_dev, z) * per_dev + q % per_dev
+    hops = (place_of(lax.axis_index("ex")) - place_of(q // per_dev) + len(RING)) % len(RING)
+    slot = jnp.zeros_like(hops)
+    for k, h in enumerate(HOPS):
+        slot = jnp.where(hops == h, k, slot)
+    place = slot * per_dev + q % per_dev
     rows = lax.broadcasted_iota(jnp.int32, (total, q.shape[1]), 0)
     chosen = jnp.where(rows == place, 1.0, 0.0).astype(BF16)
     hi, mid, low = split3(summed)
@@ -168,6 +196,14 @@
 
 def vmem():
     return pl.BlockSpec(memory_space=pltpu.VMEM)
+
+
+def place_of(index):
+    return (index % 2) * 2 + index // 2
+
+
+def shift(x, hops):
+    return lax.ppermute(x, "ex", [(RING[i], RING[(i + hops) % len(RING)]) for i in range(len(RING))])
 
 
 def swap(x, axis, count, k):
@@ -193,22 +229,25 @@
             pltpu.VMEM((rank, proj_out.shape[1]), BF16),
             pltpu.SemaphoreType.DMA((4 + CHUNKS,)),
         ],
-        compiler_params=pltpu.CompilerParams(vmem_limit_bytes=56508416),
+        compiler_params=pltpu.CompilerParams(vmem_limit_bytes=16 * 1024 * 1024),
         name="project",
-    )(frame_lengths, layer_inputs, out_grads, jnp.swapaxes(proj_in, 1, 2), jnp.swapaxes(proj_out, 1, 2))
-    packets = [packet] + [swap(packet, "ex", ex_count, k) for k in range(1, ex_count)]
+    )(*[
+        pltpu.with_memory_space_constraint(x, pltpu.HBM)
+        for x in (frame_lengths, layer_inputs, out_grads, jnp.swapaxes(proj_in, 1, 2), jnp.swapaxes(proj_out, 1, 2))
+    ])
+    packets = [packet] + [shift(packet, hops) for hops in HOPS[1:]]
     share = pl.pallas_call(
         functools.partial(solve_kernel, rank * rank, per_dev, rank),
         out_shape=jax.ShapeDtypeStruct((per_dev, total), F32),
         in_specs=[vmem()] * ex_count,
         out_specs=vmem(),
-        scratch_shapes=[pltpu.VMEM((per_dev, total), F32)],
+        scratch_shapes=[pltpu.VMEM((per_dev, total), F32), pltpu.VMEM((rank * rank // 128 + 1, total, 128), F32)],
         compiler_params=pltpu.CompilerParams(vmem_limit_bytes=16 * 1024 * 1024),
         name="solve",
     )(*packets)
     shares = [share] + [swap(share, "layer", layer_count, k) for k in range(1, layer_count)]
     scores = pl.pallas_call(
-        functools.partial(score_kernel, ex_count, per_dev),
+        functools.partial(score_kernel, per_dev),
         out_shape=jax.ShapeDtypeStruct((per_dev, query_ids.shape[0]), F32),
         in_specs=[vmem()] * 5,
         out_specs=vmem(),

time: 27.5 us -> 41.1 us (1.49)
  Pallas kernels: 12.9 us -> 27.8 us
  local copies, waits for them, and re-layouts: 0.67 us -> 0.01 us
  waiting for transfers between devices: 6.09 us -> 5.54 us
    pallas_call x1, Pallas kernels: 9.95 us -> 24.8 us  [small_device(): pl.pallas_call(functools.partial(solve_kernel, rank * rank, per_dev, rank...]
    ppermute x6 -> x3, starting transfers between devices: 7.68 us -> 1.92 us  [swap(): return lax.ppermute(x, axis, [(i, i ^ k) for i in range(count)])]
    ppermute x0 -> x3, starting transfers between devices: none -> 5.67 us  [shift(): lax.ppermute(x, 'ex', [(RING[i], RING[(i + hops) % len(RING)]) for i in r...]
    ppermute x6 -> x3, waiting for transfers between devices: 6.09 us -> 1.87 us  [swap(): return lax.ppermute(x, axis, [(i, i ^ k) for i in range(count)])]
    ppermute x0 -> x3, waiting for transfers between devices: none -> 3.67 us  [shift(): lax.ppermute(x, 'ex', [(RING[i], RING[(i + hops) % len(RING)]) for i in r...]
    unnamed x4 -> x2, local copies, waits for them, and re-layouts: 0.67 us -> 0.01 us
  transfers between devices with their start and end apart: 6 -> 6, of which waited for: 4 -> 5; matrix products, arithmetic and copies ran while one was open for 0% -> 0% of each run, Pallas kernels for 0% -> 0%
where the time goes in v2:
time: 41.1 us; the launch traced here: 41 us
  Pallas kernels  27.8 us (68%)
  starting transfers between devices  7.59 us (18%)
  waiting for transfers between devices  5.54 us (13%)
    pallas_call x1, Pallas kernels, small_device(): pl.pallas_call(functools.partial(solve_kernel, rank * rank, per_dev, rank...  24.8 us
    ppermute x3, starting transfers between devices, shift(): lax.ppermute(x, 'ex', [(RING[i], RING[(i + hops) % len(RING)]) for i in r...  5.67 us
    ppermute x3, waiting for transfers between devices, shift(): lax.ppermute(x, 'ex', [(RING[i], RING[(i + hops) % len(RING)]) for i in r...  3.67 us
    pallas_call x1, Pallas kernels, small_device(): pl.pallas_call(project_kernel, out_shape=jax.ShapeDtypeStruct((2 * rank +...  2.23 us
    ppermute x3, starting transfers between devices, swap(): return lax.ppermute(x, axis, [(i, i ^ k) for i in range(count)])  1.92 us
    ppermute x3, waiting for transfers between devices, swap(): return lax.ppermute(x, axis, [(i, i ^ k) for i in range(count)])  1.87 us
  transfers between devices with their start and end apart: 6, of which 5 were waited for; matrix products, arithmetic and copies ran while one was open for 0% of the time, Pallas kernels for 0%

profile of v2, /device:TPU:0, one launch (start us, length us, event | category | flops | bytes accessed | tf_op | source)
XLA Modules:
  0.0 41.0 jit_solution(7961396974128892285)
XLA Ops:
  0.0 0.0 copy-start
  0.0 2.2 %project.1.refs_0_ = f32[72,128]{1,0:T(8,128)S(1)} custom-call(s32[1,16]{1,0:T(1,128)} %lens_hbm.1, bf16[1,128,1280]{2,1,0:T(8,128)(2,1)} %li_ref.1, bf16[1,128,5120]{2,1,0:T(8,128)(2,1)} %og_ref.1, bf16[1,32,1280]{2,1,0:T(8,128)(2,1)} %bitcast.6, bf16[1,32,5120]{2,1,0:T(8,128)(2,1)} %bitcast.5), custom_call_target="tpu_custom_call" | custom-call | tf_op jit(solution)/shard_map/project/pallas_call | solution.py:219
  2.2 4.1 %collective-permute-start.2 = (f32[72,128]{1,0:T(8,128)S(1)}, f32[72,128]{1,0:T(8,128)S(1)}, u32[]{:S(2)}, u32[]{:S(2)}) collective-permute-start(f32[72,128]{1,0:T(8,128)S(1)} %project.1.refs_0_), channel_id=1, source_target_pairs={{0,8},{8,4},{4,12},{12,0},{1,9},{9,5},{5,13},{13,1},{2,10},{10,6},... | collective-permute-start | bytes 110600 | tf_op jit(solution)/shard_map/ppermute | solution.py:206
  6.3 1.1 %collective-permute-start.1 = (f32[72,128]{1,0:T(8,128)S(1)}, f32[72,128]{1,0:T(8,128)S(1)}, u32[]{:S(2)}, u32[]{:S(2)}) collective-permute-start(f32[72,128]{1,0:T(8,128)S(1)} %project.1.refs_0_), channel_id=1, source_target_pairs={{0,12},{8,0},{4,8},{12,4},{1,13},{9,1},{5,9},{13,5},{2,14},{10,2},... | collective-permute-start | bytes 110600 | tf_op jit(solution)/shard_map/ppermute | solution.py:206
  7.4 0.5 %collective-permute-start = (f32[72,128]{1,0:T(8,128)S(1)}, f32[72,128]{1,0:T(8,128)S(1)}, u32[]{:S(2)}, u32[]{:S(2)}) collective-permute-start(f32[72,128]{1,0:T(8,128)S(1)} %project.1.refs_0_), channel_id=1, source_target_pairs={{0,4},{8,12},{4,0},{12,8},{1,5},{9,13},{5,1},{13,9},{2,6},{10,14},... | collective-permute-start | bytes 110600 | tf_op jit(solution)/shard_map/ppermute | solution.py:206
  7.9 1.4 %collective-permute-done.2.refs_3_ = f32[72,128]{1,0:T(8,128)S(1)} collective-permute-done((f32[72,128]{1,0:T(8,128)S(1)}, f32[72,128]{1,0:T(8,128)S(1)}, u32[]{:S(2)}, u32[]{:S(2)}) %collective-permute-start.2) | collective-permute-done | bytes 36896 | tf_op jit(solution)/shard_map/ppermute | solution.py:206
  9.3 1.9 %collective-permute-done.1.refs_2_ = f32[72,128]{1,0:T(8,128)S(1)} collective-permute-done((f32[72,128]{1,0:T(8,128)S(1)}, f32[72,128]{1,0:T(8,128)S(1)}, u32[]{:S(2)}, u32[]{:S(2)}) %collective-permute-start.1) | collective-permute-done | bytes 36896 | tf_op jit(solution)/shard_map/ppermute | solution.py:206
  11.2 0.4 collective-permute-done.refs_1_
  11.6 24.8 %solve.1.a_ref = f32[16,64]{1,0:T(8,128)S(1)} custom-call(f32[72,128]{1,0:T(8,128)S(1)} %project.1.refs_0_, f32[72,128]{1,0:T(8,128)S(1)} %collective-permute-done.refs_1_, f32[72,128]{1,0:T(8,128)S(1)} %collective-permute-done.1.refs_2_, f32[72,128]{1,0:T(8,128)S(1)} %collective-permute-done.2.refs_3_), custom_call_target="tpu_custom_call" | custom-call | tf_op jit(solution)/shard_map/solve/pallas_call | solution.py:239
  36.4 0.1 collective-permute-start.5
  36.5 1.6 %collective-permute-start.4 = (f32[16,64]{1,0:T(8,128)S(1)}, f32[16,64]{1,0:T(8,128)S(1)}, u32[]{:S(2)}, u32[]{:S(2)}) collective-permute-start(f32[16,64]{1,0:T(8,128)S(1)} %solve.1.a_ref), channel_id=1, source_target_pairs={{0,2},{1,3},{2,0},{3,1},{4,6},{5,7},{6,4},{7,5},{8,10},{9,11},{10,... | collective-permute-start | bytes 12296 | tf_op jit(solution)/shard_map/ppermute | solution.py:210
  38.0 0.3 collective-permute-start.3
  38.3 1.3 %collective-permute-done.5.d_ref = f32[16,64]{1,0:T(8,128)S(1)} collective-permute-done((f32[16,64]{1,0:T(8,128)S(1)}, f32[16,64]{1,0:T(8,128)S(1)}, u32[]{:S(2)}, u32[]{:S(2)}) %collective-permute-start.5) | collective-permute-done | bytes 4128 | tf_op jit(solution)/shard_map/ppermute | solution.py:210
  39.6 0.6 %collective-permute-done.4.c_ref = f32[16,64]{1,0:T(8,128)S(1)} collective-permute-done((f32[16,64]{1,0:T(8,128)S(1)}, f32[16,64]{1,0:T(8,128)S(1)}, u32[]{:S(2)}, u32[]{:S(2)}) %collective-permute-start.4) | collective-permute-done | bytes 4128 | tf_op jit(solution)/shard_map/ppermute | solution.py:210
  40.2 0.0 collective-permute-done.3.b_ref
  40.2 0.0 copy-done
  40.2 0.8 %score.1 = f32[16,256]{1,0:T(8,128)} custom-call(f32[16,64]{1,0:T(8,128)S(1)} %solve.1.a_ref, f32[16,64]{1,0:T(8,128)S(1)} %collective-permute-done.3.b_ref, f32[16,64]{1,0:T(8,128)S(1)} %collective-permute-done.4.c_ref, f32[16,64]{1,0:T(8,128)S(1)} %collective-permute-done.5.d_ref, s32[1,256]{1,0:T(1,128)S(1)} %bitcast.4), custom_call_target="tpu_custom_call" | custom-call | tf_op jit(solution)/shard_map/score/pallas_call | solution.py:249
Async XLA Ops:
  0.0 40.2 %copy-start = (s32[256]{0:T(256)S(1)}, s32[256]{0:T(256)}, u32[]{:S(2)}) copy-start(s32[256]{0:T(256)} %param.11) | copy-start | bytes 3076
  2.2 7.0 %collective-permute-start.2 = (f32[72,128]{1,0:T(8,128)S(1)}, f32[72,128]{1,0:T(8,128)S(1)}, u32[]{:S(2)}, u32[]{:S(2)}) collective-permute-start(f32[72,128]{1,0:T(8,128)S(1)} %project.1.refs_0_), channel_id=1, source_target_pairs={{0,8},{8,4},{4,12},{12,0},{1,9},{9,5},{5,13},{13,1},{2,10},{10,6},... | collective-permute-start | bytes 110600 | tf_op jit(solution)/shard_map/ppermute | solution.py:206
  6.3 4.9 %collective-permute-start.1 = (f32[72,128]{1,0:T(8,128)S(1)}, f32[72,128]{1,0:T(8,128)S(1)}, u32[]{:S(2)}, u32[]{:S(2)}) collective-permute-start(f32[72,128]{1,0:T(8,128)S(1)} %project.1.refs_0_), channel_id=1, source_target_pairs={{0,12},{8,0},{4,8},{12,4},{1,13},{9,1},{5,9},{13,5},{2,14},{10,2},... | collective-permute-start | bytes 110600 | tf_op jit(solution)/shard_map/ppermute | solution.py:206
  7.4 4.2 %collective-permute-start = (f32[72,128]{1,0:T(8,128)S(1)}, f32[72,128]{1,0:T(8,128)S(1)}, u32[]{:S(2)}, u32[]{:S(2)}) collective-permute-start(f32[72,128]{1,0:T(8,128)S(1)} %project.1.refs_0_), channel_id=1, source_target_pairs={{0,4},{8,12},{4,0},{12,8},{1,5},{9,13},{5,1},{13,9},{2,6},{10,14},... | collective-permute-start | bytes 110600 | tf_op jit(solution)/shard_map/ppermute | solution.py:206
  36.4 3.2 %collective-permute-start.5 = (f32[16,64]{1,0:T(8,128)S(1)}, f32[16,64]{1,0:T(8,128)S(1)}, u32[]{:S(2)}, u32[]{:S(2)}) collective-permute-start(f32[16,64]{1,0:T(8,128)S(1)} %solve.1.a_ref), channel_id=1, source_target_pairs={{0,3},{1,2},{2,1},{3,0},{4,7},{5,6},{6,5},{7,4},{8,11},{9,10},{10,... | collective-permute-start | bytes 12296 | tf_op jit(solution)/shard_map/ppermute | solution.py:210
  36.5 3.7 %collective-permute-start.4 = (f32[16,64]{1,0:T(8,128)S(1)}, f32[16,64]{1,0:T(8,128)S(1)}, u32[]{:S(2)}, u32[]{:S(2)}) collective-permute-start(f32[16,64]{1,0:T(8,128)S(1)} %solve.1.a_ref), channel_id=1, source_target_pairs={{0,2},{1,3},{2,0},{3,1},{4,6},{5,7},{6,4},{7,5},{8,10},{9,11},{10,... | collective-permute-start | bytes 12296 | tf_op jit(solution)/shard_map/ppermute | solution.py:210
  38.0 2.2 %collective-permute-start.3 = (f32[16,64]{1,0:T(8,128)S(1)}, f32[16,64]{1,0:T(8,128)S(1)}, u32[]{:S(2)}, u32[]{:S(2)}) collective-permute-start(f32[16,64]{1,0:T(8,128)S(1)} %solve.1.a_ref), channel_id=1, source_target_pairs={{0,1},{1,0},{2,3},{3,2},{4,5},{5,4},{6,7},{7,6},{8,9},{9,8},{10,11... | collective-permute-start | bytes 12296 | tf_op jit(solution)/shard_map/ppermute | solution.py:210

commit v3 on v2

--- a/solution.py
+++ b/solution.py
@@ -11,7 +11,8 @@
 BF16 = jnp.bfloat16
 CHUNKS = 4
 RING = (0, 2, 1, 3)
-HOPS = (0, 2, 3, 1)
+HOPS = (0, 1, 2, 3)
+EARLY = 2
 
 
 def nt(a, b):
@@ -122,27 +123,55 @@
     return jnp.where(row == lane, 1.0, 0.0)[:per_dev, :total] - inverse[:per_dev, :total]
 
 
+def terms(packets, lo, rank):
+    hi, low = split2(jnp.concatenate([p[lo:lo + rank, :] for p in packets], axis=1))
+    return jnp.concatenate([hi, hi, low], axis=0), jnp.concatenate([hi, low, hi], axis=0)
+
+
+def members(packet, first, total, rank):
+    row = lax.broadcasted_iota(jnp.int32, (total, packet.shape[1]), 0).astype(F32)
+    return jnp.where(packet[2 * rank:2 * rank + 1, :] + float(first) == row, 1.0, 0.0)
+
+
+def early_kernel(per_dev, rank, query_ref, *refs):
+    packets, (out_ref, chosen_ref, left_o_ref, left_i_ref) = refs[:-4], refs[-4:]
+    total = out_ref.shape[0]
+    chosen_ref[...] = chosen_of(total, per_dev, query_ref[...])
+    member = jnp.concatenate([members(p, k * per_dev, total, rank) for k, p in enumerate(packets)], axis=1).astype(BF16)
+    left_o, right_o = terms(packets, 0, rank)
+    left_i, right_i = terms(packets, rank, rank)
+    left_o, left_i = left_o.T, left_i.T
+    left_o_ref[...] = left_o
+    left_i_ref[...] = left_i
+    hi, low = split2(nn(left_o, right_o) * nn(left_i, right_i))
+    hi, low = split2(nn(member, low) + nn(member, hi))
+    out_ref[...] = nt(low, member) + nt(hi, member)
+
+
+def extend(known, left_o, left_i, packets, member, skip, rank):
+    frames = packets[0].shape[1]
+    first, late = member[:, :skip * frames], member[:, skip * frames:]
+    late_o, right_o = terms(packets[skip:], 0, rank)
+    late_i, right_i = terms(packets[skip:], rank, rank)
+    cross_hi, cross_low = split2(nn(left_o, right_o) * nn(left_i, right_i))
+    own_hi, own_low = split2(tn(late_o, right_o) * tn(late_i, right_i))
+    cross = nn(first, cross_low) + nn(first, cross_hi)
+    hi, low = split2(cross + (nn(late, own_low) + nn(late, own_hi)))
+    columns = nt(low, late) + nt(hi, late)
+    hi, low = split2(cross)
+    return known + (columns + (nt(late, low) + nt(late, hi)))
+
+
 def solve_kernel(width, per_dev, rank, *refs):
-    packets, out_ref, s_ref, v_ref = refs[:-3], refs[-3], refs[-2], refs[-1]
+    early_ref, left_o_ref, left_i_ref = refs[:3]
+    packets, (out_ref, s_ref, v_ref) = refs[3:-3], refs[-3:]
     frames = packets[0].shape[1]
     count = len(packets)
     total = count * per_dev
 
-    def terms(lo):
-        x = jnp.concatenate([p[lo:lo + rank, :] for p in packets], axis=1)
-        hi, low = split2(x)
-        return jnp.concatenate([hi, hi, low], axis=0), jnp.concatenate([hi, low, hi], axis=0)
-
-    left_o, right_o = terms(0)
-    left_i, right_i = terms(rank)
-    row = lax.broadcasted_iota(jnp.int32, (total, frames), 0).astype(F32)
-    membership = jnp.concatenate(
-        [jnp.where(p[2 * rank:2 * rank + 1, :] + float(k * per_dev) == row, 1.0, 0.0) for k, p in enumerate(packets)], axis=1
-    )
+    membership = jnp.concatenate([members(p, k * per_dev, total, rank) for k, p in enumerate(packets)], axis=1)
     member = membership.astype(BF16)
-    hi, low = split2(tn(left_o, right_o) * tn(left_i, right_i))
-    hi, low = split2(nt(low, member) + nt(hi, member))
-    kernel = nn(member, low) + nn(member, hi)
+    kernel = extend(early_ref[...], left_o_ref[...], left_i_ref[...], packets, member, EARLY, rank)
 
     ids0 = lax.broadcasted_iota(jnp.int32, (total, total), 0)
     ids1 = lax.broadcasted_iota(jnp.int32, (total, total), 1)
@@ -179,18 +208,19 @@
     out_ref[...] = s_ref[...]
 
 
-def score_kernel(per_dev, a_ref, b_ref, c_ref, d_ref, q_ref, out_ref):
-    summed = (a_ref[...] + b_ref[...]) + (c_ref[...] + d_ref[...])
-    total = summed.shape[1]
-    q = q_ref[...]
+def chosen_of(total, per_dev, q):
     hops = (place_of(lax.axis_index("ex")) - place_of(q // per_dev) + len(RING)) % len(RING)
     slot = jnp.zeros_like(hops)
     for k, h in enumerate(HOPS):
         slot = jnp.where(hops == h, k, slot)
     place = slot * per_dev + q % per_dev
     rows = lax.broadcasted_iota(jnp.int32, (total, q.shape[1]), 0)
-    chosen = jnp.where(rows == place, 1.0, 0.0).astype(BF16)
-    hi, mid, low = split3(summed)
+    return jnp.where(rows == place, 1.0, 0.0).astype(BF16)
+
+
+def score_kernel(a_ref, b_ref, c_ref, d_ref, chosen_ref, out_ref):
+    chosen = chosen_ref[...]
+    hi, mid, low = split3((a_ref[...] + b_ref[...]) + (c_ref[...] + d_ref[...]))
     out_ref[...] = (nn(low, chosen) + nn(mid, chosen)) + nn(hi, chosen)
 
 
@@ -236,24 +266,34 @@
         for x in (frame_lengths, layer_inputs, out_grads, jnp.swapaxes(proj_in, 1, 2), jnp.swapaxes(proj_out, 1, 2))
     ])
     packets = [packet] + [shift(packet, hops) for hops in HOPS[1:]]
+    lefts = jax.ShapeDtypeStruct((EARLY * frames, 3 * rank), BF16)
+    early, chosen, left_o, left_i = pl.pallas_call(
+        functools.partial(early_kernel, per_dev, rank),
+        out_shape=(jax.ShapeDtypeStruct((total, total), F32), jax.ShapeDtypeStruct((total, query_ids.shape[0]), BF16), lefts, lefts),
+        in_specs=[vmem()] * (1 + EARLY),
+        out_specs=(vmem(),) * 4,
+        compiler_params=pltpu.CompilerParams(vmem_limit_bytes=16 * 1024 * 1024),
+        cost_estimate=pl.CostEstimate(flops=10**6, bytes_accessed=10**5, transcendentals=0),
+        name="early",
+    )(query_ids.reshape(1, -1), *packets[:EARLY])
     share = pl.pallas_call(
         functools.partial(solve_kernel, rank * rank, per_dev, rank),
         out_shape=jax.ShapeDtypeStruct((per_dev, total), F32),
-        in_specs=[vmem()] * ex_count,
+        in_specs=[vmem()] * (ex_count + 3),
         out_specs=vmem(),
         scratch_shapes=[pltpu.VMEM((per_dev, total), F32), pltpu.VMEM((rank * rank // 128 + 1, total, 128), F32)],
         compiler_params=pltpu.CompilerParams(vmem_limit_bytes=16 * 1024 * 1024),
         name="solve",
-    )(*packets)
+    )(early, left_o, left_i, *packets)
     shares = [share] + [swap(share, "layer", layer_count, k) for k in range(1, layer_count)]
     scores = pl.pallas_call(
-        functools.partial(score_kernel, per_dev),
+        score_kernel,
         out_shape=jax.ShapeDtypeStruct((per_dev, query_ids.shape[0]), F32),
         in_specs=[vmem()] * 5,
         out_specs=vmem(),
         compiler_params=pltpu.CompilerParams(vmem_limit_bytes=16 * 1024 * 1024),
         name="score",
-    )(*shares, query_ids.reshape(1, -1))
+    )(*shares, chosen)
     return scores.T
 
 

time: 41.1 us -> 40.5 us (0.985)
  waiting for transfers between devices: 5.54 us -> 5 us
    pallas_call x1, Pallas kernels: 24.8 us -> 24.2 us  [small_device(): pl.pallas_call(functools.partial(solve_kernel, rank * rank, per_dev, rank...]
    ppermute x3, waiting for transfers between devices: 3.67 us -> 3.13 us  [shift(): lax.ppermute(x, 'ex', [(RING[i], RING[(i + hops) % len(RING)]) for i in r...]
    pallas_call x1 -> x2, Pallas kernels: 0.77 us -> 1.28 us  [the longest x1 0.74 us: small_device(): pl.pallas_call(score_kernel, out_shape=jax.ShapeDtypeStruct((per_dev, que...]
  transfers between devices with their start and end apart: 6 -> 6, of which waited for: 5 -> 5; matrix products, arithmetic and copies ran while one was open for 0% -> 0% of each run, Pallas kernels for 0% -> 1%
where the time goes in v3:
time: 40.5 us; the launch traced here: 40.3 us
  Pallas kernels  27.7 us (68%)
  starting transfers between devices  7.59 us (19%)
  waiting for transfers between devices  5 us (12%)
    pallas_call x1, Pallas kernels, small_device(): pl.pallas_call(functools.partial(solve_kernel, rank * rank, per_dev, rank...  24.2 us
    ppermute x3, starting transfers between devices, shift(): lax.ppermute(x, 'ex', [(RING[i], RING[(i + hops) % len(RING)]) for i in r...  5.67 us
    ppermute x3, waiting for transfers between devices, shift(): lax.ppermute(x, 'ex', [(RING[i], RING[(i + hops) % len(RING)]) for i in r...  3.13 us
    pallas_call x1, Pallas kernels, small_device(): pl.pallas_call(project_kernel, out_shape=jax.ShapeDtypeStruct((2 * rank +...  2.23 us
    ppermute x3, starting transfers between devices, swap(): return lax.ppermute(x, axis, [(i, i ^ k) for i in range(count)])  1.92 us
    ppermute x3, waiting for transfers between devices, swap(): return lax.ppermute(x, axis, [(i, i ^ k) for i in range(count)])  1.87 us
  transfers between devices with their start and end apart: 6, of which 5 were waited for; matrix products, arithmetic and copies ran while one was open for 0% of the time, Pallas kernels for 1%

profile of v3, /device:TPU:0, one launch (start us, length us, event | category | flops | bytes accessed | tf_op | source)
XLA Modules:
  0.0 40.3 jit_solution(1833016205594587685)
XLA Ops:
  0.0 0.0 copy-start
  0.0 2.2 %project.1.refs_0_.refs_3_ = f32[72,128]{1,0:T(8,128)S(1)} custom-call(s32[1,16]{1,0:T(1,128)} %lens_hbm.1, bf16[1,128,1280]{2,1,0:T(8,128)(2,1)} %li_ref.1, bf16[1,128,5120]{2,1,0:T(8,128)(2,1)} %og_ref.1, bf16[1,32,1280]{2,1,0:T(8,128)(2,1)} %bitcast.6, bf16[1,32,5120]{2,1,0:T(8,128)(2,1)} %bitcast.5), custom_call_target="tpu_custom_call" | custom-call | tf_op jit(solution)/shard_map/project/pallas_call | solution.py:249
  2.2 4.1 %collective-permute-start = (f32[72,128]{1,0:T(8,128)S(1)}, f32[72,128]{1,0:T(8,128)S(1)}, u32[]{:S(2)}, u32[]{:S(2)}) collective-permute-start(f32[72,128]{1,0:T(8,128)S(1)} %project.1.refs_0_.refs_3_), channel_id=1, source_target_pairs={{0,8},{8,4},{4,12},{12,0},{1,9},{9,5},{5,13},{13,1},{2,10},{10,6},... | collective-permute-start | bytes 110600 | tf_op jit(solution)/shard_map/ppermute | solution.py:236
  6.3 1.1 %collective-permute-start.2 = (f32[72,128]{1,0:T(8,128)S(1)}, f32[72,128]{1,0:T(8,128)S(1)}, u32[]{:S(2)}, u32[]{:S(2)}) collective-permute-start(f32[72,128]{1,0:T(8,128)S(1)} %project.1.refs_0_.refs_3_), channel_id=1, source_target_pairs={{0,12},{8,0},{4,8},{12,4},{1,13},{9,1},{5,9},{13,5},{2,14},{10,2},... | collective-permute-start | bytes 110600 | tf_op jit(solution)/shard_map/ppermute | solution.py:236
  7.4 0.5 %collective-permute-start.1 = (f32[72,128]{1,0:T(8,128)S(1)}, f32[72,128]{1,0:T(8,128)S(1)}, u32[]{:S(2)}, u32[]{:S(2)}) collective-permute-start(f32[72,128]{1,0:T(8,128)S(1)} %project.1.refs_0_.refs_3_), channel_id=1, source_target_pairs={{0,4},{8,12},{4,0},{12,8},{1,5},{9,13},{5,1},{13,9},{2,6},{10,14},... | collective-permute-start | bytes 110600 | tf_op jit(solution)/shard_map/ppermute | solution.py:236
  7.9 1.4 %collective-permute-done.refs_1_.refs_4_ = f32[72,128]{1,0:T(8,128)S(1)} collective-permute-done((f32[72,128]{1,0:T(8,128)S(1)}, f32[72,128]{1,0:T(8,128)S(1)}, u32[]{:S(2)}, u32[]{:S(2)}) %collective-permute-start) | collective-permute-done | bytes 36896 | tf_op jit(solution)/shard_map/ppermute | solution.py:236
  9.3 0.0 copy-done
  9.3 0.5 %early.1 = (f32[64,64]{1,0:T(8,128)S(1)}, bf16[64,256]{1,0:T(8,128)(2,1)S(1)}, bf16[256,96]{1,0:T(8,128)(2,1)S(1)}, bf16[256,96]{1,0:T(8,128)(2,1)S(1)}) custom-call(s32[1,256]{1,0:T(1,128)S(1)} %bitcast.4, f32[72,128]{1,0:T(8,128)S(1)} %project.1.refs_0_.refs_3_, f32[72,128]{1,0:T(8,128)S(1)} %collective-permute-done.refs_1_.refs_4_), custom_call_target="tpu_custom_call" | custom-call | flops 1000000 | bytes 100000 | tf_op jit(solution)/shard_map/early/pallas_call | solution.py:270
  9.8 1.4 %collective-permute-done.2.refs_6_ = f32[72,128]{1,0:T(8,128)S(1)} collective-permute-done((f32[72,128]{1,0:T(8,128)S(1)}, f32[72,128]{1,0:T(8,128)S(1)}, u32[]{:S(2)}, u32[]{:S(2)}) %collective-permute-start.2) | collective-permute-done | bytes 36896 | tf_op jit(solution)/shard_map/ppermute | solution.py:236
  11.2 0.4 collective-permute-done.1.refs_5_
  11.6 24.2 %solve.1.a_ref = f32[16,64]{1,0:T(8,128)S(1)} custom-call(f32[64,64]{1,0:T(8,128)S(1)} %get-tuple-element.9.refs_0_, bf16[256,96]{1,0:T(8,128)(2,1)S(1)} %get-tuple-element.10.refs_1_, bf16[256,96]{1,0:T(8,128)(2,1)S(1)} %get-tuple-element.11.refs_2_, f32[72,128]{1,0:T(8,128)S(1)} %project.1.refs_0_.refs_3_, ...), custom_call_target="tpu_custom_call" | custom-call | tf_op jit(solution)/shard_map/solve/pallas_call | solution.py:279
  35.8 0.1 collective-permute-start.5
  35.9 1.6 %collective-permute-start.4 = (f32[16,64]{1,0:T(8,128)S(1)}, f32[16,64]{1,0:T(8,128)S(1)}, u32[]{:S(2)}, u32[]{:S(2)}) collective-permute-start(f32[16,64]{1,0:T(8,128)S(1)} %solve.1.a_ref), channel_id=1, source_target_pairs={{0,2},{1,3},{2,0},{3,1},{4,6},{5,7},{6,4},{7,5},{8,10},{9,11},{10,... | collective-permute-start | bytes 12296 | tf_op jit(solution)/shard_map/ppermute | solution.py:240
  37.4 0.3 collective-permute-start.3
  37.7 1.3 %collective-permute-done.5.d_ref = f32[16,64]{1,0:T(8,128)S(1)} collective-permute-done((f32[16,64]{1,0:T(8,128)S(1)}, f32[16,64]{1,0:T(8,128)S(1)}, u32[]{:S(2)}, u32[]{:S(2)}) %collective-permute-start.5) | collective-permute-done | bytes 4128 | tf_op jit(solution)/shard_map/ppermute | solution.py:240
  39.0 0.6 %collective-permute-done.4.c_ref = f32[16,64]{1,0:T(8,128)S(1)} collective-permute-done((f32[16,64]{1,0:T(8,128)S(1)}, f32[16,64]{1,0:T(8,128)S(1)}, u32[]{:S(2)}, u32[]{:S(2)}) %collective-permute-start.4) | collective-permute-done | bytes 4128 | tf_op jit(solution)/shard_map/ppermute | solution.py:240
  39.6 0.0 collective-permute-done.3.b_ref
  39.6 0.7 %score.1 = f32[16,256]{1,0:T(8,128)} custom-call(f32[16,64]{1,0:T(8,128)S(1)} %solve.1.a_ref, f32[16,64]{1,0:T(8,128)S(1)} %collective-permute-done.3.b_ref, f32[16,64]{1,0:T(8,128)S(1)} %collective-permute-done.4.c_ref, f32[16,64]{1,0:T(8,128)S(1)} %collective-permute-done.5.d_ref, bf16[64,256]{1,0:T(8,128)(2,1)S(1)} %get-tuple-element.12.chosen_ref), custom_call_target="tpu_custom_call" | custom-call | tf_op jit(solution)/shard_map/score/pallas_call | solution.py:289
Async XLA Ops:
  0.0 9.3 %copy-start = (s32[256]{0:T(256)S(1)}, s32[256]{0:T(256)}, u32[]{:S(2)}) copy-start(s32[256]{0:T(256)} %param.11) | copy-start | bytes 3076
  2.2 7.0 %collective-permute-start = (f32[72,128]{1,0:T(8,128)S(1)}, f32[72,128]{1,0:T(8,128)S(1)}, u32[]{:S(2)}, u32[]{:S(2)}) collective-permute-start(f32[72,128]{1,0:T(8,128)S(1)} %project.1.refs_0_.refs_3_), channel_id=1, source_target_pairs={{0,8},{8,4},{4,12},{12,0},{1,9},{9,5},{5,13},{13,1},{2,10},{10,6},... | collective-permute-start | bytes 110600 | tf_op jit(solution)/shard_map/ppermute | solution.py:236
  6.3 4.9 %collective-permute-start.2 = (f32[72,128]{1,0:T(8,128)S(1)}, f32[72,128]{1,0:T(8,128)S(1)}, u32[]{:S(2)}, u32[]{:S(2)}) collective-permute-start(f32[72,128]{1,0:T(8,128)S(1)} %project.1.refs_0_.refs_3_), channel_id=1, source_target_pairs={{0,12},{8,0},{4,8},{12,4},{1,13},{9,1},{5,9},{13,5},{2,14},{10,2},... | collective-permute-start | bytes 110600 | tf_op jit(solution)/shard_map/ppermute | solution.py:236
  7.4 4.2 %collective-permute-start.1 = (f32[72,128]{1,0:T(8,128)S(1)}, f32[72,128]{1,0:T(8,128)S(1)}, u32[]{:S(2)}, u32[]{:S(2)}) collective-permute-start(f32[72,128]{1,0:T(8,128)S(1)} %project.1.refs_0_.refs_3_), channel_id=1, source_target_pairs={{0,4},{8,12},{4,0},{12,8},{1,5},{9,13},{5,1},{13,9},{2,6},{10,14},... | collective-permute-start | bytes 110600 | tf_op jit(solution)/shard_map/ppermute | solution.py:236
  35.8 3.2 %collective-permute-start.5 = (f32[16,64]{1,0:T(8,128)S(1)}, f32[16,64]{1,0:T(8,128)S(1)}, u32[]{:S(2)}, u32[]{:S(2)}) collective-permute-start(f32[16,64]{1,0:T(8,128)S(1)} %solve.1.a_ref), channel_id=1, source_target_pairs={{0,3},{1,2},{2,1},{3,0},{4,7},{5,6},{6,5},{7,4},{8,11},{9,10},{10,... | collective-permute-start | bytes 12296 | tf_op jit(solution)/shard_map/ppermute | solution.py:240
  35.9 3.7 %collective-permute-start.4 = (f32[16,64]{1,0:T(8,128)S(1)}, f32[16,64]{1,0:T(8,128)S(1)}, u32[]{:S(2)}, u32[]{:S(2)}) collective-permute-start(f32[16,64]{1,0:T(8,128)S(1)} %solve.1.a_ref), channel_id=1, source_target_pairs={{0,2},{1,3},{2,0},{3,1},{4,6},{5,7},{6,4},{7,5},{8,10},{9,11},{10,... | collective-permute-start | bytes 12296 | tf_op jit(solution)/shard_map/ppermute | solution.py:240
  37.4 2.2 %collective-permute-start.3 = (f32[16,64]{1,0:T(8,128)S(1)}, f32[16,64]{1,0:T(8,128)S(1)}, u32[]{:S(2)}, u32[]{:S(2)}) collective-permute-start(f32[16,64]{1,0:T(8,128)S(1)} %solve.1.a_ref), channel_id=1, source_target_pairs={{0,1},{1,0},{2,3},{3,2},{4,5},{5,4},{6,7},{7,6},{8,9},{9,8},{10,11... | collective-permute-start | bytes 12296 | tf_op jit(solution)/shard_map/ppermute | solution.py:240

commit v4 on v3

--- a/solution.py
+++ b/solution.py
@@ -43,7 +43,7 @@
 def mm(a, b):
     ah, al = split2(a)
     bh, bl = split2(b)
-    return nn(ah, bh) + (nn(ah, bl) + nn(al, bh))
+    return (nn(ah, bl) + nn(al, bh)) + nn(ah, bh)
 
 
 def exact(a, b, dims):
@@ -177,17 +177,18 @@
     ids1 = lax.broadcasted_iota(jnp.int32, (total, total), 1)
     diagonal = ids0 == ids1
     eye = jnp.where(diagonal, 1.0, 0.0)
-    damp = jnp.sum(jnp.where(diagonal, kernel, 0.0), keepdims=True) * (0.1 / width)
-    scale = jnp.sum(jnp.where(diagonal, kernel, 0.0), axis=0, keepdims=True) + damp
-    ratio = damp / scale
-    column = jnp.sum(jnp.where(diagonal, ratio, 0.0), axis=1, keepdims=True)
-    e1 = jnp.where(diagonal, 0.0, -kernel / scale)
+    own = jnp.sum(jnp.where(diagonal, kernel, 0.0), axis=0, keepdims=True)
+    damp = jnp.sum(own, axis=1, keepdims=True) * (0.1 / width)
+    scale = own + damp
+    inverse = 1.0 / scale
+    column = jnp.sum(jnp.where(diagonal, damp * inverse, 0.0), axis=1, keepdims=True)
+    e1 = jnp.where(diagonal, 0.0, kernel) * -inverse
     mine = e1[:per_dev] + eye[:per_dev]
     e2 = mm(e1, e1)
+    e4 = mm(e2, e2)
     mine = mine + mm(mine, e2)
-    e4 = mm(e2, e2)
+    e8 = mm(e4, e4)
     mine = mine + mm(mine, e4)
-    e8 = mm(e4, e4)
     mine = mine + mm(mine, e8)
     squares = e8 * e8
     left = jnp.sum(squares * column)

time: 40.5 us -> 40.4 us (level)
  no operation moved by 1% of the time
where the time goes in v4:
time: 40.4 us; the launch traced here: 40.3 us
  Pallas kernels  27.7 us (69%)
  starting transfers between devices  7.59 us (19%)
  waiting for transfers between devices  5 us (12%)
    pallas_call x1, Pallas kernels, small_device(): pl.pallas_call(functools.partial(solve_kernel, rank * rank, per_dev, rank...  24.2 us
    ppermute x3, starting transfers between devices, shift(): lax.ppermute(x, 'ex', [(RING[i], RING[(i + hops) % len(RING)]) for i in r...  5.67 us
    ppermute x3, waiting for transfers between devices, shift(): lax.ppermute(x, 'ex', [(RING[i], RING[(i + hops) % len(RING)]) for i in r...  3.13 us
    pallas_call x1, Pallas kernels, small_device(): pl.pallas_call(project_kernel, out_shape=jax.ShapeDtypeStruct((2 * rank +...  2.23 us
    ppermute x3, starting transfers between devices, swap(): return lax.ppermute(x, axis, [(i, i ^ k) for i in range(count)])  1.92 us
    ppermute x3, waiting for transfers between devices, swap(): return lax.ppermute(x, axis, [(i, i ^ k) for i in range(count)])  1.87 us
  transfers between devices with their start and end apart: 6, of which 5 were waited for; matrix products, arithmetic and copies ran while one was open for 0% of the time, Pallas kernels for 1%

profile of v4, /device:TPU:0, one launch (start us, length us, event | category | flops | bytes accessed | tf_op | source)
XLA Modules:
  0.0 40.3 jit_solution(6309077049611807240)
XLA Ops:
  0.0 0.0 copy-start
  0.0 2.2 %project.1.refs_0_.refs_3_ = f32[72,128]{1,0:T(8,128)S(1)} custom-call(s32[1,16]{1,0:T(1,128)} %lens_hbm.1, bf16[1,128,1280]{2,1,0:T(8,128)(2,1)} %li_ref.1, bf16[1,128,5120]{2,1,0:T(8,128)(2,1)} %og_ref.1, bf16[1,32,1280]{2,1,0:T(8,128)(2,1)} %bitcast.6, bf16[1,32,5120]{2,1,0:T(8,128)(2,1)} %bitcast.5), custom_call_target="tpu_custom_call" | custom-call | tf_op jit(solution)/shard_map/project/pallas_call | solution.py:250
  2.2 4.1 %collective-permute-start = (f32[72,128]{1,0:T(8,128)S(1)}, f32[72,128]{1,0:T(8,128)S(1)}, u32[]{:S(2)}, u32[]{:S(2)}) collective-permute-start(f32[72,128]{1,0:T(8,128)S(1)} %project.1.refs_0_.refs_3_), channel_id=1, source_target_pairs={{0,8},{8,4},{4,12},{12,0},{1,9},{9,5},{5,13},{13,1},{2,10},{10,6},... | collective-permute-start | bytes 110600 | tf_op jit(solution)/shard_map/ppermute | solution.py:237
  6.3 1.1 %collective-permute-start.2 = (f32[72,128]{1,0:T(8,128)S(1)}, f32[72,128]{1,0:T(8,128)S(1)}, u32[]{:S(2)}, u32[]{:S(2)}) collective-permute-start(f32[72,128]{1,0:T(8,128)S(1)} %project.1.refs_0_.refs_3_), channel_id=1, source_target_pairs={{0,12},{8,0},{4,8},{12,4},{1,13},{9,1},{5,9},{13,5},{2,14},{10,2},... | collective-permute-start | bytes 110600 | tf_op jit(solution)/shard_map/ppermute | solution.py:237
  7.4 0.5 %collective-permute-start.1 = (f32[72,128]{1,0:T(8,128)S(1)}, f32[72,128]{1,0:T(8,128)S(1)}, u32[]{:S(2)}, u32[]{:S(2)}) collective-permute-start(f32[72,128]{1,0:T(8,128)S(1)} %project.1.refs_0_.refs_3_), channel_id=1, source_target_pairs={{0,4},{8,12},{4,0},{12,8},{1,5},{9,13},{5,1},{13,9},{2,6},{10,14},... | collective-permute-start | bytes 110600 | tf_op jit(solution)/shard_map/ppermute | solution.py:237
  7.9 1.4 %collective-permute-done.refs_1_.refs_4_ = f32[72,128]{1,0:T(8,128)S(1)} collective-permute-done((f32[72,128]{1,0:T(8,128)S(1)}, f32[72,128]{1,0:T(8,128)S(1)}, u32[]{:S(2)}, u32[]{:S(2)}) %collective-permute-start) | collective-permute-done | bytes 36896 | tf_op jit(solution)/shard_map/ppermute | solution.py:237
  9.3 0.0 copy-done
  9.3 0.5 %early.1 = (f32[64,64]{1,0:T(8,128)S(1)}, bf16[64,256]{1,0:T(8,128)(2,1)S(1)}, bf16[256,96]{1,0:T(8,128)(2,1)S(1)}, bf16[256,96]{1,0:T(8,128)(2,1)S(1)}) custom-call(s32[1,256]{1,0:T(1,128)S(1)} %bitcast.4, f32[72,128]{1,0:T(8,128)S(1)} %project.1.refs_0_.refs_3_, f32[72,128]{1,0:T(8,128)S(1)} %collective-permute-done.refs_1_.refs_4_), custom_call_target="tpu_custom_call" | custom-call | flops 1000000 | bytes 100000 | tf_op jit(solution)/shard_map/early/pallas_call | solution.py:271
  9.8 1.4 %collective-permute-done.2.refs_6_ = f32[72,128]{1,0:T(8,128)S(1)} collective-permute-done((f32[72,128]{1,0:T(8,128)S(1)}, f32[72,128]{1,0:T(8,128)S(1)}, u32[]{:S(2)}, u32[]{:S(2)}) %collective-permute-start.2) | collective-permute-done | bytes 36896 | tf_op jit(solution)/shard_map/ppermute | solution.py:237
  11.2 0.4 collective-permute-done.1.refs_5_
  11.6 24.2 %solve.1.a_ref = f32[16,64]{1,0:T(8,128)S(1)} custom-call(f32[64,64]{1,0:T(8,128)S(1)} %get-tuple-element.9.refs_0_, bf16[256,96]{1,0:T(8,128)(2,1)S(1)} %get-tuple-element.10.refs_1_, bf16[256,96]{1,0:T(8,128)(2,1)S(1)} %get-tuple-element.11.refs_2_, f32[72,128]{1,0:T(8,128)S(1)} %project.1.refs_0_.refs_3_, ...), custom_call_target="tpu_custom_call" | custom-call | tf_op jit(solution)/shard_map/solve/pallas_call | solution.py:280
  35.7 0.1 collective-permute-start.5
  35.8 1.6 %collective-permute-start.4 = (f32[16,64]{1,0:T(8,128)S(1)}, f32[16,64]{1,0:T(8,128)S(1)}, u32[]{:S(2)}, u32[]{:S(2)}) collective-permute-start(f32[16,64]{1,0:T(8,128)S(1)} %solve.1.a_ref), channel_id=1, source_target_pairs={{0,2},{1,3},{2,0},{3,1},{4,6},{5,7},{6,4},{7,5},{8,10},{9,11},{10,... | collective-permute-start | bytes 12296 | tf_op jit(solution)/shard_map/ppermute | solution.py:241
  37.4 0.3 collective-permute-start.3
  37.7 1.3 %collective-permute-done.5.d_ref = f32[16,64]{1,0:T(8,128)S(1)} collective-permute-done((f32[16,64]{1,0:T(8,128)S(1)}, f32[16,64]{1,0:T(8,128)S(1)}, u32[]{:S(2)}, u32[]{:S(2)}) %collective-permute-start.5) | collective-permute-done | bytes 4128 | tf_op jit(solution)/shard_map/ppermute | solution.py:241
  38.9 0.6 %collective-permute-done.4.c_ref = f32[16,64]{1,0:T(8,128)S(1)} collective-permute-done((f32[16,64]{1,0:T(8,128)S(1)}, f32[16,64]{1,0:T(8,128)S(1)}, u32[]{:S(2)}, u32[]{:S(2)}) %collective-permute-start.4) | collective-permute-done | bytes 4128 | tf_op jit(solution)/shard_map/ppermute | solution.py:241
  39.5 0.0 collective-permute-done.3.b_ref
  39.5 0.7 %score.1 = f32[16,256]{1,0:T(8,128)} custom-call(f32[16,64]{1,0:T(8,128)S(1)} %solve.1.a_ref, f32[16,64]{1,0:T(8,128)S(1)} %collective-permute-done.3.b_ref, f32[16,64]{1,0:T(8,128)S(1)} %collective-permute-done.4.c_ref, f32[16,64]{1,0:T(8,128)S(1)} %collective-permute-done.5.d_ref, bf16[64,256]{1,0:T(8,128)(2,1)S(1)} %get-tuple-element.12.chosen_ref), custom_call_target="tpu_custom_call" | custom-call | tf_op jit(solution)/shard_map/score/pallas_call | solution.py:290
Async XLA Ops:
  0.0 9.3 %copy-start = (s32[256]{0:T(256)S(1)}, s32[256]{0:T(256)}, u32[]{:S(2)}) copy-start(s32[256]{0:T(256)} %param.11) | copy-start | bytes 3076
  2.2 7.0 %collective-permute-start = (f32[72,128]{1,0:T(8,128)S(1)}, f32[72,128]{1,0:T(8,128)S(1)}, u32[]{:S(2)}, u32[]{:S(2)}) collective-permute-start(f32[72,128]{1,0:T(8,128)S(1)} %project.1.refs_0_.refs_3_), channel_id=1, source_target_pairs={{0,8},{8,4},{4,12},{12,0},{1,9},{9,5},{5,13},{13,1},{2,10},{10,6},... | collective-permute-start | bytes 110600 | tf_op jit(solution)/shard_map/ppermute | solution.py:237
  6.3 4.9 %collective-permute-start.2 = (f32[72,128]{1,0:T(8,128)S(1)}, f32[72,128]{1,0:T(8,128)S(1)}, u32[]{:S(2)}, u32[]{:S(2)}) collective-permute-start(f32[72,128]{1,0:T(8,128)S(1)} %project.1.refs_0_.refs_3_), channel_id=1, source_target_pairs={{0,12},{8,0},{4,8},{12,4},{1,13},{9,1},{5,9},{13,5},{2,14},{10,2},... | collective-permute-start | bytes 110600 | tf_op jit(solution)/shard_map/ppermute | solution.py:237
  7.4 4.2 %collective-permute-start.1 = (f32[72,128]{1,0:T(8,128)S(1)}, f32[72,128]{1,0:T(8,128)S(1)}, u32[]{:S(2)}, u32[]{:S(2)}) collective-permute-start(f32[72,128]{1,0:T(8,128)S(1)} %project.1.refs_0_.refs_3_), channel_id=1, source_target_pairs={{0,4},{8,12},{4,0},{12,8},{1,5},{9,13},{5,1},{13,9},{2,6},{10,14},... | collective-permute-start | bytes 110600 | tf_op jit(solution)/shard_map/ppermute | solution.py:237
  35.7 3.2 %collective-permute-start.5 = (f32[16,64]{1,0:T(8,128)S(1)}, f32[16,64]{1,0:T(8,128)S(1)}, u32[]{:S(2)}, u32[]{:S(2)}) collective-permute-start(f32[16,64]{1,0:T(8,128)S(1)} %solve.1.a_ref), channel_id=1, source_target_pairs={{0,3},{1,2},{2,1},{3,0},{4,7},{5,6},{6,5},{7,4},{8,11},{9,10},{10,... | collective-permute-start | bytes 12296 | tf_op jit(solution)/shard_map/ppermute | solution.py:241
  35.8 3.7 %collective-permute-start.4 = (f32[16,64]{1,0:T(8,128)S(1)}, f32[16,64]{1,0:T(8,128)S(1)}, u32[]{:S(2)}, u32[]{:S(2)}) collective-permute-start(f32[16,64]{1,0:T(8,128)S(1)} %solve.1.a_ref), channel_id=1, source_target_pairs={{0,2},{1,3},{2,0},{3,1},{4,6},{5,7},{6,4},{7,5},{8,10},{9,11},{10,... | collective-permute-start | bytes 12296 | tf_op jit(solution)/shard_map/ppermute | solution.py:241
  37.4 2.2 %collective-permute-start.3 = (f32[16,64]{1,0:T(8,128)S(1)}, f32[16,64]{1,0:T(8,128)S(1)}, u32[]{:S(2)}, u32[]{:S(2)}) collective-permute-start(f32[16,64]{1,0:T(8,128)S(1)} %solve.1.a_ref), channel_id=1, source_target_pairs={{0,1},{1,0},{2,3},{3,2},{4,5},{5,4},{6,7},{7,6},{8,9},{9,8},{10,11... | collective-permute-start | bytes 12296 | tf_op jit(solution)/shard_map/ppermute | solution.py:241

commit v5 on v4

--- a/solution.py
+++ b/solution.py
@@ -13,6 +13,7 @@
 RING = (0, 2, 1, 3)
 HOPS = (0, 1, 2, 3)
 EARLY = 2
+RELAX = 0.92
 
 
 def nt(a, b):
@@ -182,7 +183,7 @@
     scale = own + damp
     inverse = 1.0 / scale
     column = jnp.sum(jnp.where(diagonal, damp * inverse, 0.0), axis=1, keepdims=True)
-    e1 = jnp.where(diagonal, 0.0, kernel) * -inverse
+    e1 = jnp.where(diagonal, 1.0 - RELAX, kernel * (inverse * -RELAX))
     mine = e1[:per_dev] + eye[:per_dev]
     e2 = mm(e1, e1)
     e4 = mm(e2, e2)
@@ -193,14 +194,14 @@
     squares = e8 * e8
     left = jnp.sum(squares * column)
     spread = jnp.sum(squares * column * (scale / damp))
-    good = (left <= 1e-5) & (spread <= 0.005)
-    s_ref[...] = eye[:per_dev] - column[:per_dev] * mine
+    good = (left <= 2e-6) & (spread <= 0.005)
+    s_ref[...] = eye[:per_dev] - RELAX * column[:per_dev] * mine
 
     @pl.when(jnp.logical_not(good))
     def _():
         e16 = mm(e8, e8)
-        s_ref[...] = eye[:per_dev] - column[:per_dev] * (mine + mm(mine, e16))
-        near = (jnp.sum(e16 * e16 * column) <= 1e-5) & (spread <= 0.05)
+        s_ref[...] = eye[:per_dev] - RELAX * column[:per_dev] * (mine + mm(mine, e16))
+        near = (jnp.sum(e16 * e16 * column) <= 2e-6) & (spread <= 0.05)
 
         @pl.when(jnp.logical_not(near))
         def _():

time: 40.4 us -> 40.4 us (level)
  no operation moved by 1% of the time
where the time goes in v5:
time: 40.4 us; the launch traced here: 40.3 us
  Pallas kernels  27.7 us (69%)
  starting transfers between devices  7.58 us (19%)
  waiting for transfers between devices  5 us (12%)
    pallas_call x1, Pallas kernels, small_device(): pl.pallas_call(functools.partial(solve_kernel, rank * rank, per_dev, rank...  24.2 us
    ppermute x3, starting transfers between devices, shift(): lax.ppermute(x, 'ex', [(RING[i], RING[(i + hops) % len(RING)]) for i in r...  5.67 us
    ppermute x3, waiting for transfers between devices, shift(): lax.ppermute(x, 'ex', [(RING[i], RING[(i + hops) % len(RING)]) for i in r...  3.13 us
    pallas_call x1, Pallas kernels, small_device(): pl.pallas_call(project_kernel, out_shape=jax.ShapeDtypeStruct((2 * rank +...  2.23 us
    ppermute x3, starting transfers between devices, swap(): return lax.ppermute(x, axis, [(i, i ^ k) for i in range(count)])  1.91 us
    ppermute x3, waiting for transfers between devices, swap(): return lax.ppermute(x, axis, [(i, i ^ k) for i in range(count)])  1.87 us
  transfers between devices with their start and end apart: 6, of which 5 were waited for; matrix products, arithmetic and copies ran while one was open for 0% of the time, Pallas kernels for 1%

profile of v5, /device:TPU:0, one launch (start us, length us, event | category | flops | bytes accessed | tf_op | source)
XLA Modules:
  0.0 40.3 jit_solution(5714057545150582431)
XLA Ops:
  0.0 0.0 copy-start
  0.0 2.2 %project.1.refs_0_.refs_3_ = f32[72,128]{1,0:T(8,128)S(1)} custom-call(s32[1,16]{1,0:T(1,128)} %lens_hbm.1, bf16[1,128,1280]{2,1,0:T(8,128)(2,1)} %li_ref.1, bf16[1,128,5120]{2,1,0:T(8,128)(2,1)} %og_ref.1, bf16[1,32,1280]{2,1,0:T(8,128)(2,1)} %bitcast.6, bf16[1,32,5120]{2,1,0:T(8,128)(2,1)} %bitcast.5), custom_call_target="tpu_custom_call" | custom-call | tf_op jit(solution)/shard_map/project/pallas_call | solution.py:251
  2.2 4.1 %collective-permute-start = (f32[72,128]{1,0:T(8,128)S(1)}, f32[72,128]{1,0:T(8,128)S(1)}, u32[]{:S(2)}, u32[]{:S(2)}) collective-permute-start(f32[72,128]{1,0:T(8,128)S(1)} %project.1.refs_0_.refs_3_), channel_id=1, source_target_pairs={{0,8},{8,4},{4,12},{12,0},{1,9},{9,5},{5,13},{13,1},{2,10},{10,6},... | collective-permute-start | bytes 110600 | tf_op jit(solution)/shard_map/ppermute | solution.py:238
  6.3 1.1 %collective-permute-start.2 = (f32[72,128]{1,0:T(8,128)S(1)}, f32[72,128]{1,0:T(8,128)S(1)}, u32[]{:S(2)}, u32[]{:S(2)}) collective-permute-start(f32[72,128]{1,0:T(8,128)S(1)} %project.1.refs_0_.refs_3_), channel_id=1, source_target_pairs={{0,12},{8,0},{4,8},{12,4},{1,13},{9,1},{5,9},{13,5},{2,14},{10,2},... | collective-permute-start | bytes 110600 | tf_op jit(solution)/shard_map/ppermute | solution.py:238
  7.4 0.5 %collective-permute-start.1 = (f32[72,128]{1,0:T(8,128)S(1)}, f32[72,128]{1,0:T(8,128)S(1)}, u32[]{:S(2)}, u32[]{:S(2)}) collective-permute-start(f32[72,128]{1,0:T(8,128)S(1)} %project.1.refs_0_.refs_3_), channel_id=1, source_target_pairs={{0,4},{8,12},{4,0},{12,8},{1,5},{9,13},{5,1},{13,9},{2,6},{10,14},... | collective-permute-start | bytes 110600 | tf_op jit(solution)/shard_map/ppermute | solution.py:238
  7.9 1.4 %collective-permute-done.refs_1_.refs_4_ = f32[72,128]{1,0:T(8,128)S(1)} collective-permute-done((f32[72,128]{1,0:T(8,128)S(1)}, f32[72,128]{1,0:T(8,128)S(1)}, u32[]{:S(2)}, u32[]{:S(2)}) %collective-permute-start) | collective-permute-done | bytes 36896 | tf_op jit(solution)/shard_map/ppermute | solution.py:238
  9.3 0.0 copy-done
  9.3 0.5 %early.1 = (f32[64,64]{1,0:T(8,128)S(1)}, bf16[64,256]{1,0:T(8,128)(2,1)S(1)}, bf16[256,96]{1,0:T(8,128)(2,1)S(1)}, bf16[256,96]{1,0:T(8,128)(2,1)S(1)}) custom-call(s32[1,256]{1,0:T(1,128)S(1)} %bitcast.4, f32[72,128]{1,0:T(8,128)S(1)} %project.1.refs_0_.refs_3_, f32[72,128]{1,0:T(8,128)S(1)} %collective-permute-done.refs_1_.refs_4_), custom_call_target="tpu_custom_call" | custom-call | flops 1000000 | bytes 100000 | tf_op jit(solution)/shard_map/early/pallas_call | solution.py:272
  9.8 1.4 %collective-permute-done.2.refs_6_ = f32[72,128]{1,0:T(8,128)S(1)} collective-permute-done((f32[72,128]{1,0:T(8,128)S(1)}, f32[72,128]{1,0:T(8,128)S(1)}, u32[]{:S(2)}, u32[]{:S(2)}) %collective-permute-start.2) | collective-permute-done | bytes 36896 | tf_op jit(solution)/shard_map/ppermute | solution.py:238
  11.2 0.4 collective-permute-done.1.refs_5_
  11.6 24.2 %solve.1.a_ref = f32[16,64]{1,0:T(8,128)S(1)} custom-call(f32[64,64]{1,0:T(8,128)S(1)} %get-tuple-element.9.refs_0_, bf16[256,96]{1,0:T(8,128)(2,1)S(1)} %get-tuple-element.10.refs_1_, bf16[256,96]{1,0:T(8,128)(2,1)S(1)} %get-tuple-element.11.refs_2_, f32[72,128]{1,0:T(8,128)S(1)} %project.1.refs_0_.refs_3_, ...), custom_call_target="tpu_custom_call" | custom-call | tf_op jit(solution)/shard_map/solve/pallas_call | solution.py:281
  35.7 0.1 collective-permute-start.5
  35.8 0.1 collective-permute-start.4
  35.9 1.8 %collective-permute-start.3 = (f32[16,64]{1,0:T(8,128)S(1)}, f32[16,64]{1,0:T(8,128)S(1)}, u32[]{:S(2)}, u32[]{:S(2)}) collective-permute-start(f32[16,64]{1,0:T(8,128)S(1)} %solve.1.a_ref), channel_id=1, source_target_pairs={{0,1},{1,0},{2,3},{3,2},{4,5},{5,4},{6,7},{7,6},{8,9},{9,8},{10,11... | collective-permute-start | bytes 12296 | tf_op jit(solution)/shard_map/ppermute | solution.py:242
  37.7 1.2 %collective-permute-done.5.d_ref = f32[16,64]{1,0:T(8,128)S(1)} collective-permute-done((f32[16,64]{1,0:T(8,128)S(1)}, f32[16,64]{1,0:T(8,128)S(1)}, u32[]{:S(2)}, u32[]{:S(2)}) %collective-permute-start.5) | collective-permute-done | bytes 4128 | tf_op jit(solution)/shard_map/ppermute | solution.py:242
  38.9 0.7 %collective-permute-done.4.c_ref = f32[16,64]{1,0:T(8,128)S(1)} collective-permute-done((f32[16,64]{1,0:T(8,128)S(1)}, f32[16,64]{1,0:T(8,128)S(1)}, u32[]{:S(2)}, u32[]{:S(2)}) %collective-permute-start.4) | collective-permute-done | bytes 4128 | tf_op jit(solution)/shard_map/ppermute | solution.py:242
  39.5 0.0 collective-permute-done.3.b_ref
  39.5 0.7 %score.1 = f32[16,256]{1,0:T(8,128)} custom-call(f32[16,64]{1,0:T(8,128)S(1)} %solve.1.a_ref, f32[16,64]{1,0:T(8,128)S(1)} %collective-permute-done.3.b_ref, f32[16,64]{1,0:T(8,128)S(1)} %collective-permute-done.4.c_ref, f32[16,64]{1,0:T(8,128)S(1)} %collective-permute-done.5.d_ref, bf16[64,256]{1,0:T(8,128)(2,1)S(1)} %get-tuple-element.12.chosen_ref), custom_call_target="tpu_custom_call" | custom-call | tf_op jit(solution)/shard_map/score/pallas_call | solution.py:291
Async XLA Ops:
  0.0 9.3 %copy-start = (s32[256]{0:T(256)S(1)}, s32[256]{0:T(256)}, u32[]{:S(2)}) copy-start(s32[256]{0:T(256)} %param.11) | copy-start | bytes 3076
  2.2 7.0 %collective-permute-start = (f32[72,128]{1,0:T(8,128)S(1)}, f32[72,128]{1,0:T(8,128)S(1)}, u32[]{:S(2)}, u32[]{:S(2)}) collective-permute-start(f32[72,128]{1,0:T(8,128)S(1)} %project.1.refs_0_.refs_3_), channel_id=1, source_target_pairs={{0,8},{8,4},{4,12},{12,0},{1,9},{9,5},{5,13},{13,1},{2,10},{10,6},... | collective-permute-start | bytes 110600 | tf_op jit(solution)/shard_map/ppermute | solution.py:238
  6.3 4.9 %collective-permute-start.2 = (f32[72,128]{1,0:T(8,128)S(1)}, f32[72,128]{1,0:T(8,128)S(1)}, u32[]{:S(2)}, u32[]{:S(2)}) collective-permute-start(f32[72,128]{1,0:T(8,128)S(1)} %project.1.refs_0_.refs_3_), channel_id=1, source_target_pairs={{0,12},{8,0},{4,8},{12,4},{1,13},{9,1},{5,9},{13,5},{2,14},{10,2},... | collective-permute-start | bytes 110600 | tf_op jit(solution)/shard_map/ppermute | solution.py:238
  7.4 4.2 %collective-permute-start.1 = (f32[72,128]{1,0:T(8,128)S(1)}, f32[72,128]{1,0:T(8,128)S(1)}, u32[]{:S(2)}, u32[]{:S(2)}) collective-permute-start(f32[72,128]{1,0:T(8,128)S(1)} %project.1.refs_0_.refs_3_), channel_id=1, source_target_pairs={{0,4},{8,12},{4,0},{12,8},{1,5},{9,13},{5,1},{13,9},{2,6},{10,14},... | collective-permute-start | bytes 110600 | tf_op jit(solution)/shard_map/ppermute | solution.py:238
  35.7 3.1 %collective-permute-start.5 = (f32[16,64]{1,0:T(8,128)S(1)}, f32[16,64]{1,0:T(8,128)S(1)}, u32[]{:S(2)}, u32[]{:S(2)}) collective-permute-start(f32[16,64]{1,0:T(8,128)S(1)} %solve.1.a_ref), channel_id=1, source_target_pairs={{0,3},{1,2},{2,1},{3,0},{4,7},{5,6},{6,5},{7,4},{8,11},{9,10},{10,... | collective-permute-start | bytes 12296 | tf_op jit(solution)/shard_map/ppermute | solution.py:242
  35.8 3.7 %collective-permute-start.4 = (f32[16,64]{1,0:T(8,128)S(1)}, f32[16,64]{1,0:T(8,128)S(1)}, u32[]{:S(2)}, u32[]{:S(2)}) collective-permute-start(f32[16,64]{1,0:T(8,128)S(1)} %solve.1.a_ref), channel_id=1, source_target_pairs={{0,2},{1,3},{2,0},{3,1},{4,6},{5,7},{6,4},{7,5},{8,10},{9,11},{10,... | collective-permute-start | bytes 12296 | tf_op jit(solution)/shard_map/ppermute | solution.py:242
  35.9 3.6 %collective-permute-start.3 = (f32[16,64]{1,0:T(8,128)S(1)}, f32[16,64]{1,0:T(8,128)S(1)}, u32[]{:S(2)}, u32[]{:S(2)}) collective-permute-start(f32[16,64]{1,0:T(8,128)S(1)} %solve.1.a_ref), channel_id=1, source_target_pairs={{0,1},{1,0},{2,3},{3,2},{4,5},{5,4},{6,7},{7,6},{8,9},{9,8},{10,11... | collective-permute-start | bytes 12296 | tf_op jit(solution)/shard_map/ppermute | solution.py:242

commit v6 on v5

--- a/solution.py
+++ b/solution.py
@@ -135,12 +135,13 @@
 
 
 def early_kernel(per_dev, rank, query_ref, *refs):
-    packets, (out_ref, chosen_ref, left_o_ref, left_i_ref) = refs[:-4], refs[-4:]
+    packets, (out_ref, chosen_ref, left_o_ref, left_i_ref, first_ref) = refs[:-5], refs[-5:]
     total = out_ref.shape[0]
     chosen_ref[...] = chosen_of(total, per_dev, query_ref[...])
     member = jnp.concatenate([members(p, k * per_dev, total, rank) for k, p in enumerate(packets)], axis=1).astype(BF16)
     left_o, right_o = terms(packets, 0, rank)
     left_i, right_i = terms(packets, rank, rank)
+    first_ref[...] = member
     left_o, left_i = left_o.T, left_i.T
     left_o_ref[...] = left_o
     left_i_ref[...] = left_i
@@ -164,14 +165,14 @@
 
 
 def solve_kernel(width, per_dev, rank, *refs):
-    early_ref, left_o_ref, left_i_ref = refs[:3]
-    packets, (out_ref, s_ref, v_ref) = refs[3:-3], refs[-3:]
+    early_ref, left_o_ref, left_i_ref, first_ref = refs[:4]
+    packets, (out_ref, v_ref) = refs[4:-2], refs[-2:]
     frames = packets[0].shape[1]
     count = len(packets)
     total = count * per_dev
 
-    membership = jnp.concatenate([members(p, k * per_dev, total, rank) for k, p in enumerate(packets)], axis=1)
-    member = membership.astype(BF16)
+    late = [members(p, k * per_dev, total, rank) for k, p in list(enumerate(packets))[EARLY:]]
+    member = jnp.concatenate([first_ref[...]] + [part.astype(BF16) for part in late], axis=1)
     kernel = extend(early_ref[...], left_o_ref[...], left_i_ref[...], packets, member, EARLY, rank)
 
     ids0 = lax.broadcasted_iota(jnp.int32, (total, total), 0)
@@ -195,19 +196,17 @@
     left = jnp.sum(squares * column)
     spread = jnp.sum(squares * column * (scale / damp))
     good = (left <= 2e-6) & (spread <= 0.005)
-    s_ref[...] = eye[:per_dev] - RELAX * column[:per_dev] * mine
+    out_ref[...] = eye[:per_dev] - RELAX * column[:per_dev] * mine
 
     @pl.when(jnp.logical_not(good))
     def _():
         e16 = mm(e8, e8)
-        s_ref[...] = eye[:per_dev] - RELAX * column[:per_dev] * (mine + mm(mine, e16))
+        out_ref[...] = eye[:per_dev] - RELAX * column[:per_dev] * (mine + mm(mine, e16))
         near = (jnp.sum(e16 * e16 * column) <= 2e-6) & (spread <= 0.05)
 
         @pl.when(jnp.logical_not(near))
         def _():
-            s_ref[...] = orthogonal_shares(width, per_dev, rank, packets, membership, v_ref)
-
-    out_ref[...] = s_ref[...]
+            out_ref[...] = orthogonal_shares(width, per_dev, rank, packets, member.astype(F32), v_ref)
 
 
 def chosen_of(total, per_dev, q):
@@ -269,11 +268,11 @@
     ])
     packets = [packet] + [shift(packet, hops) for hops in HOPS[1:]]
     lefts = jax.ShapeDtypeStruct((EARLY * frames, 3 * rank), BF16)
-    early, chosen, left_o, left_i = pl.pallas_call(
+    early, chosen, left_o, left_i, first = pl.pallas_call(
         functools.partial(early_kernel, per_dev, rank),
-        out_shape=(jax.ShapeDtypeStruct((total, total), F32), jax.ShapeDtypeStruct((total, query_ids.shape[0]), BF16), lefts, lefts),
+        out_shape=(jax.ShapeDtypeStruct((total, total), F32), jax.ShapeDtypeStruct((total, query_ids.shape[0]), BF16), lefts, lefts, jax.ShapeDtypeStruct((total, EARLY * frames), BF16)),
         in_specs=[vmem()] * (1 + EARLY),
-        out_specs=(vmem(),) * 4,
+        out_specs=(vmem(),) * 5,
         compiler_params=pltpu.CompilerParams(vmem_limit_bytes=16 * 1024 * 1024),
         cost_estimate=pl.CostEstimate(flops=10**6, bytes_accessed=10**5, transcendentals=0),
         name="early",
@@ -281,12 +280,12 @@
     share = pl.pallas_call(
         functools.partial(solve_kernel, rank * rank, per_dev, rank),
         out_shape=jax.ShapeDtypeStruct((per_dev, total), F32),
-        in_specs=[vmem()] * (ex_count + 3),
+        in_specs=[vmem()] * (ex_count + 4),
         out_specs=vmem(),
-        scratch_shapes=[pltpu.VMEM((per_dev, total), F32), pltpu.VMEM((rank * rank // 128 + 1, total, 128), F32)],
+        scratch_shapes=[pltpu.VMEM((rank * rank // 128 + 1, total, 128), F32)],
         compiler_params=pltpu.CompilerParams(vmem_limit_bytes=16 * 1024 * 1024),
         name="solve",
-    )(early, left_o, left_i, *packets)
+    )(early, left_o, left_i, first, *packets)
     shares = [share] + [swap(share, "layer", layer_count, k) for k in range(1, layer_count)]
     scores = pl.pallas_call(
         score_kernel,

time: 40.4 us -> 40.2 us (level)
  no operation moved by 1% of the time
where the time goes in v6:
time: 40.2 us; the launch traced here: 40.3 us
  Pallas kernels  27.7 us (69%)
  starting transfers between devices  7.59 us (19%)
  waiting for transfers between devices  5 us (12%)
    pallas_call x1, Pallas kernels, small_device(): pl.pallas_call(functools.partial(solve_kernel, rank * rank, per_dev, rank...  24.2 us
    ppermute x3, starting transfers between devices, shift(): lax.ppermute(x, 'ex', [(RING[i], RING[(i + hops) % len(RING)]) for i in r...  5.67 us
    ppermute x3, waiting for transfers between devices, shift(): lax.ppermute(x, 'ex', [(RING[i], RING[(i + hops) % len(RING)]) for i in r...  3.13 us
    pallas_call x1, Pallas kernels, small_device(): pl.pallas_call(project_kernel, out_shape=jax.ShapeDtypeStruct((2 * rank +...  2.23 us
    ppermute x3, starting transfers between devices, swap(): return lax.ppermute(x, axis, [(i, i ^ k) for i in range(count)])  1.92 us
    ppermute x3, waiting for transfers between devices, swap(): return lax.ppermute(x, axis, [(i, i ^ k) for i in range(count)])  1.87 us
  transfers between devices with their start and end apart: 6, of which 5 were waited for; matrix products, arithmetic and copies ran while one was open for 0% of the time, Pallas kernels for 1%

profile of v6, /device:TPU:0, one launch (start us, length us, event | category | flops | bytes accessed | tf_op | source)
XLA Modules:
  0.0 40.3 jit_solution(3732303732268468867)
XLA Ops:
  0.0 0.0 copy-start
  0.0 2.2 %project.1.refs_0_.refs_4_ = f32[72,128]{1,0:T(8,128)S(1)} custom-call(s32[1,16]{1,0:T(1,128)} %lens_hbm.1, bf16[1,128,1280]{2,1,0:T(8,128)(2,1)} %li_ref.1, bf16[1,128,5120]{2,1,0:T(8,128)(2,1)} %og_ref.1, bf16[1,32,1280]{2,1,0:T(8,128)(2,1)} %bitcast.6, bf16[1,32,5120]{2,1,0:T(8,128)(2,1)} %bitcast.5), custom_call_target="tpu_custom_call" | custom-call | tf_op jit(solution)/shard_map/project/pallas_call | solution.py:250
  2.2 4.1 %collective-permute-start = (f32[72,128]{1,0:T(8,128)S(1)}, f32[72,128]{1,0:T(8,128)S(1)}, u32[]{:S(2)}, u32[]{:S(2)}) collective-permute-start(f32[72,128]{1,0:T(8,128)S(1)} %project.1.refs_0_.refs_4_), channel_id=1, source_target_pairs={{0,8},{8,4},{4,12},{12,0},{1,9},{9,5},{5,13},{13,1},{2,10},{10,6},... | collective-permute-start | bytes 110600 | tf_op jit(solution)/shard_map/ppermute | solution.py:237
  6.3 1.1 %collective-permute-start.2 = (f32[72,128]{1,0:T(8,128)S(1)}, f32[72,128]{1,0:T(8,128)S(1)}, u32[]{:S(2)}, u32[]{:S(2)}) collective-permute-start(f32[72,128]{1,0:T(8,128)S(1)} %project.1.refs_0_.refs_4_), channel_id=1, source_target_pairs={{0,12},{8,0},{4,8},{12,4},{1,13},{9,1},{5,9},{13,5},{2,14},{10,2},... | collective-permute-start | bytes 110600 | tf_op jit(solution)/shard_map/ppermute | solution.py:237
  7.4 0.5 %collective-permute-start.1 = (f32[72,128]{1,0:T(8,128)S(1)}, f32[72,128]{1,0:T(8,128)S(1)}, u32[]{:S(2)}, u32[]{:S(2)}) collective-permute-start(f32[72,128]{1,0:T(8,128)S(1)} %project.1.refs_0_.refs_4_), channel_id=1, source_target_pairs={{0,4},{8,12},{4,0},{12,8},{1,5},{9,13},{5,1},{13,9},{2,6},{10,14},... | collective-permute-start | bytes 110600 | tf_op jit(solution)/shard_map/ppermute | solution.py:237
  7.9 1.4 %collective-permute-done.refs_1_.refs_5_ = f32[72,128]{1,0:T(8,128)S(1)} collective-permute-done((f32[72,128]{1,0:T(8,128)S(1)}, f32[72,128]{1,0:T(8,128)S(1)}, u32[]{:S(2)}, u32[]{:S(2)}) %collective-permute-start) | collective-permute-done | bytes 36896 | tf_op jit(solution)/shard_map/ppermute | solution.py:237
  9.3 0.0 copy-done
  9.3 0.5 %early.1 = (f32[64,64]{1,0:T(8,128)S(1)}, bf16[64,256]{1,0:T(8,128)(2,1)S(1)}, bf16[256,96]{1,0:T(8,128)(2,1)S(1)}, bf16[256,96]{1,0:T(8,128)(2,1)S(1)}, bf16[64,256]{1,0:T(8,128)(2,1)S(1)}) custom-call(s32[1,256]{1,0:T(1,128)S(1)} %bitcast.4, f32[72,128]{1,0:T(8,128)S(1)} %project.1.refs_0_.refs_4_, f32[72,128]{1,0:T(8,128)S(1)} %collective-permute-done.refs_1_.refs_5_), custom_call_target="tpu_custom_call" | custom-call | flops 1000000 | bytes 100000 | tf_op jit(solution)/shard_map/early/pallas_call | solution.py:271
  9.8 1.4 %collective-permute-done.2.refs_7_ = f32[72,128]{1,0:T(8,128)S(1)} collective-permute-done((f32[72,128]{1,0:T(8,128)S(1)}, f32[72,128]{1,0:T(8,128)S(1)}, u32[]{:S(2)}, u32[]{:S(2)}) %collective-permute-start.2) | collective-permute-done | bytes 36896 | tf_op jit(solution)/shard_map/ppermute | solution.py:237
  11.2 0.4 collective-permute-done.1.refs_6_
  11.6 24.2 %solve.1.a_ref = f32[16,64]{1,0:T(8,128)S(1)} custom-call(f32[64,64]{1,0:T(8,128)S(1)} %get-tuple-element.10.refs_0_, bf16[256,96]{1,0:T(8,128)(2,1)S(1)} %get-tuple-element.11.refs_1_, bf16[256,96]{1,0:T(8,128)(2,1)S(1)} %get-tuple-element.12.refs_2_, bf16[64,256]{1,0:T(8,128)(2,1)S(1)} %get-tuple-element.13.refs_3_, f32[72,128]{1,0:T(8,128)S(1)} %project.1.refs_0_.refs_4_, ...), custom_call_target="tpu_custom_call" | custom-call | tf_op jit(solution)/shard_map/solve/pallas_call | solution.py:280
  35.8 0.1 collective-permute-start.5
  35.9 1.6 %collective-permute-start.4 = (f32[16,64]{1,0:T(8,128)S(1)}, f32[16,64]{1,0:T(8,128)S(1)}, u32[]{:S(2)}, u32[]{:S(2)}) collective-permute-start(f32[16,64]{1,0:T(8,128)S(1)} %solve.1.a_ref), channel_id=1, source_target_pairs={{0,2},{1,3},{2,0},{3,1},{4,6},{5,7},{6,4},{7,5},{8,10},{9,11},{10,... | collective-permute-start | bytes 12296 | tf_op jit(solution)/shard_map/ppermute | solution.py:241
  37.4 0.3 collective-permute-start.3
  37.7 1.3 %collective-permute-done.5.d_ref = f32[16,64]{1,0:T(8,128)S(1)} collective-permute-done((f32[16,64]{1,0:T(8,128)S(1)}, f32[16,64]{1,0:T(8,128)S(1)}, u32[]{:S(2)}, u32[]{:S(2)}) %collective-permute-start.5) | collective-permute-done | bytes 4128 | tf_op jit(solution)/shard_map/ppermute | solution.py:241
  39.0 0.6 %collective-permute-done.4.c_ref = f32[16,64]{1,0:T(8,128)S(1)} collective-permute-done((f32[16,64]{1,0:T(8,128)S(1)}, f32[16,64]{1,0:T(8,128)S(1)}, u32[]{:S(2)}, u32[]{:S(2)}) %collective-permute-start.4) | collective-permute-done | bytes 4128 | tf_op jit(solution)/shard_map/ppermute | solution.py:241
  39.6 0.0 collective-permute-done.3.b_ref
  39.6 0.7 %score.1 = f32[16,256]{1,0:T(8,128)} custom-call(f32[16,64]{1,0:T(8,128)S(1)} %solve.1.a_ref, f32[16,64]{1,0:T(8,128)S(1)} %collective-permute-done.3.b_ref, f32[16,64]{1,0:T(8,128)S(1)} %collective-permute-done.4.c_ref, f32[16,64]{1,0:T(8,128)S(1)} %collective-permute-done.5.d_ref, bf16[64,256]{1,0:T(8,128)(2,1)S(1)} %get-tuple-element.14.chosen_ref), custom_call_target="tpu_custom_call" | custom-call | tf_op jit(solution)/shard_map/score/pallas_call | solution.py:290
Async XLA Ops:
  0.0 9.3 %copy-start = (s32[256]{0:T(256)S(1)}, s32[256]{0:T(256)}, u32[]{:S(2)}) copy-start(s32[256]{0:T(256)} %param.11) | copy-start | bytes 3076
  2.2 7.0 %collective-permute-start = (f32[72,128]{1,0:T(8,128)S(1)}, f32[72,128]{1,0:T(8,128)S(1)}, u32[]{:S(2)}, u32[]{:S(2)}) collective-permute-start(f32[72,128]{1,0:T(8,128)S(1)} %project.1.refs_0_.refs_4_), channel_id=1, source_target_pairs={{0,8},{8,4},{4,12},{12,0},{1,9},{9,5},{5,13},{13,1},{2,10},{10,6},... | collective-permute-start | bytes 110600 | tf_op jit(solution)/shard_map/ppermute | solution.py:237
  6.3 4.9 %collective-permute-start.2 = (f32[72,128]{1,0:T(8,128)S(1)}, f32[72,128]{1,0:T(8,128)S(1)}, u32[]{:S(2)}, u32[]{:S(2)}) collective-permute-start(f32[72,128]{1,0:T(8,128)S(1)} %project.1.refs_0_.refs_4_), channel_id=1, source_target_pairs={{0,12},{8,0},{4,8},{12,4},{1,13},{9,1},{5,9},{13,5},{2,14},{10,2},... | collective-permute-start | bytes 110600 | tf_op jit(solution)/shard_map/ppermute | solution.py:237
  7.4 4.2 %collective-permute-start.1 = (f32[72,128]{1,0:T(8,128)S(1)}, f32[72,128]{1,0:T(8,128)S(1)}, u32[]{:S(2)}, u32[]{:S(2)}) collective-permute-start(f32[72,128]{1,0:T(8,128)S(1)} %project.1.refs_0_.refs_4_), channel_id=1, source_target_pairs={{0,4},{8,12},{4,0},{12,8},{1,5},{9,13},{5,1},{13,9},{2,6},{10,14},... | collective-permute-start | bytes 110600 | tf_op jit(solution)/shard_map/ppermute | solution.py:237
  35.8 3.2 %collective-permute-start.5 = (f32[16,64]{1,0:T(8,128)S(1)}, f32[16,64]{1,0:T(8,128)S(1)}, u32[]{:S(2)}, u32[]{:S(2)}) collective-permute-start(f32[16,64]{1,0:T(8,128)S(1)} %solve.1.a_ref), channel_id=1, source_target_pairs={{0,3},{1,2},{2,1},{3,0},{4,7},{5,6},{6,5},{7,4},{8,11},{9,10},{10,... | collective-permute-start | bytes 12296 | tf_op jit(solution)/shard_map/ppermute | solution.py:241
  35.9 3.7 %collective-permute-start.4 = (f32[16,64]{1,0:T(8,128)S(1)}, f32[16,64]{1,0:T(8,128)S(1)}, u32[]{:S(2)}, u32[]{:S(2)}) collective-permute-start(f32[16,64]{1,0:T(8,128)S(1)} %solve.1.a_ref), channel_id=1, source_target_pairs={{0,2},{1,3},{2,0},{3,1},{4,6},{5,7},{6,4},{7,5},{8,10},{9,11},{10,... | collective-permute-start | bytes 12296 | tf_op jit(solution)/shard_map/ppermute | solution.py:241
  37.4 2.2 %collective-permute-start.3 = (f32[16,64]{1,0:T(8,128)S(1)}, f32[16,64]{1,0:T(8,128)S(1)}, u32[]{:S(2)}, u32[]{:S(2)}) collective-permute-start(f32[16,64]{1,0:T(8,128)S(1)} %solve.1.a_ref), channel_id=1, source_target_pairs={{0,1},{1,0},{2,3},{3,2},{4,5},{5,4},{6,7},{7,6},{8,9},{9,8},{10,11... | collective-permute-start | bytes 12296 | tf_op jit(solution)/shard_map/ppermute | solution.py:241

commit v7 on v6

--- a/solution.py
+++ b/solution.py
@@ -9,7 +9,7 @@
 
 F32 = jnp.float32
 BF16 = jnp.bfloat16
-CHUNKS = 4
+CUTS = (0, 1, 3, 5)
 RING = (0, 2, 1, 3)
 HOPS = (0, 1, 2, 3)
 EARLY = 2
@@ -53,15 +53,15 @@
 
 def project_kernel(lens_hbm, li_ref, og_ref, pi_ref, po_ref, out_ref, lens_ref, li_v, og_v, pi_v, po_v, sems):
     ff = og_ref.shape[2]
-    step = ff // CHUNKS
+    cuts = [ff * cut // CUTS[-1] for cut in CUTS]
+    chunks = [slice(lo, hi) for lo, hi in zip(cuts, cuts[1:])]
     copies = [
         pltpu.make_async_copy(pi_ref.at[0], pi_v, sems.at[0]),
         pltpu.make_async_copy(li_ref.at[0], li_v, sems.at[1]),
         pltpu.make_async_copy(po_ref.at[0], po_v, sems.at[2]),
         pltpu.make_async_copy(lens_hbm, lens_ref, sems.at[3]),
     ]
-    for c in range(CHUNKS):
-        cols = pl.ds(c * step, step)
+    for c, cols in enumerate(chunks):
         copies.append(pltpu.make_async_copy(og_ref.at[0, :, cols], og_v.at[:, cols], sems.at[4 + c]))
     for copy in copies:
         copy.start()
@@ -80,9 +80,9 @@
     out_ref[rank:2 * rank, :] = nt(pi_v[...], li_v[...])
     copies[2].wait()
     total = jnp.zeros((rank, frames), F32)
-    for c in range(CHUNKS):
+    for c, cols in enumerate(chunks):
         copies[4 + c].wait()
-        total = total + nt(po_v[:, c * step:(c + 1) * step], og_v[:, c * step:(c + 1) * step])
+        total = total + nt(po_v[:, cols], og_v[:, cols])
     out_ref[:rank, :] = total
 
 
@@ -258,7 +258,7 @@
             pltpu.VMEM(out_grads.shape[1:], BF16),
             pltpu.VMEM((rank, proj_in.shape[1]), BF16),
             pltpu.VMEM((rank, proj_out.shape[1]), BF16),
-            pltpu.SemaphoreType.DMA((4 + CHUNKS,)),
+            pltpu.SemaphoreType.DMA((3 + len(CUTS),)),
         ],
         compiler_params=pltpu.CompilerParams(vmem_limit_bytes=16 * 1024 * 1024),
         name="project",

time: 40.2 us -> 40.4 us (level)
  no operation moved by 1% of the time
where the time goes in v7:
time: 40.4 us; the launch traced here: 40.3 us
  Pallas kernels  27.7 us (69%)
  starting transfers between devices  7.59 us (19%)
  waiting for transfers between devices  5 us (12%)
    pallas_call x1, Pallas kernels, small_device(): pl.pallas_call(functools.partial(solve_kernel, rank * rank, per_dev, rank...  24.2 us
    ppermute x3, starting transfers between devices, shift(): lax.ppermute(x, 'ex', [(RING[i], RING[(i + hops) % len(RING)]) for i in r...  5.67 us
    ppermute x3, waiting for transfers between devices, shift(): lax.ppermute(x, 'ex', [(RING[i], RING[(i + hops) % len(RING)]) for i in r...  3.13 us
    pallas_call x1, Pallas kernels, small_device(): pl.pallas_call(project_kernel, out_shape=jax.ShapeDtypeStruct((2 * rank +...  2.19 us
    ppermute x3, starting transfers between devices, swap(): return lax.ppermute(x, axis, [(i, i ^ k) for i in range(count)])  1.92 us
    ppermute x3, waiting for transfers between devices, swap(): return lax.ppermute(x, axis, [(i, i ^ k) for i in range(count)])  1.87 us
  transfers between devices with their start and end apart: 6, of which 5 were waited for; matrix products, arithmetic and copies ran while one was open for 0% of the time, Pallas kernels for 1%

profile of v7, /device:TPU:0, one launch (start us, length us, event | category | flops | bytes accessed | tf_op | source)
XLA Modules:
  0.0 40.3 jit_solution(5569093667175178318)
XLA Ops:
  0.0 0.0 copy-start
  0.0 2.2 %project.1.refs_0_.refs_4_ = f32[72,128]{1,0:T(8,128)S(1)} custom-call(s32[1,16]{1,0:T(1,128)} %lens_hbm.1, bf16[1,128,1280]{2,1,0:T(8,128)(2,1)} %li_ref.1, bf16[1,128,5120]{2,1,0:T(8,128)(2,1)} %og_ref.1, bf16[1,32,1280]{2,1,0:T(8,128)(2,1)} %bitcast.6, bf16[1,32,5120]{2,1,0:T(8,128)(2,1)} %bitcast.5), custom_call_target="tpu_custom_call" | custom-call | tf_op jit(solution)/shard_map/project/pallas_call | solution.py:250
  2.2 4.1 %collective-permute-start = (f32[72,128]{1,0:T(8,128)S(1)}, f32[72,128]{1,0:T(8,128)S(1)}, u32[]{:S(2)}, u32[]{:S(2)}) collective-permute-start(f32[72,128]{1,0:T(8,128)S(1)} %project.1.refs_0_.refs_4_), channel_id=1, source_target_pairs={{0,8},{8,4},{4,12},{12,0},{1,9},{9,5},{5,13},{13,1},{2,10},{10,6},... | collective-permute-start | bytes 110600 | tf_op jit(solution)/shard_map/ppermute | solution.py:237
  6.3 1.1 %collective-permute-start.2 = (f32[72,128]{1,0:T(8,128)S(1)}, f32[72,128]{1,0:T(8,128)S(1)}, u32[]{:S(2)}, u32[]{:S(2)}) collective-permute-start(f32[72,128]{1,0:T(8,128)S(1)} %project.1.refs_0_.refs_4_), channel_id=1, source_target_pairs={{0,12},{8,0},{4,8},{12,4},{1,13},{9,1},{5,9},{13,5},{2,14},{10,2},... | collective-permute-start | bytes 110600 | tf_op jit(solution)/shard_map/ppermute | solution.py:237
  7.4 0.5 %collective-permute-start.1 = (f32[72,128]{1,0:T(8,128)S(1)}, f32[72,128]{1,0:T(8,128)S(1)}, u32[]{:S(2)}, u32[]{:S(2)}) collective-permute-start(f32[72,128]{1,0:T(8,128)S(1)} %project.1.refs_0_.refs_4_), channel_id=1, source_target_pairs={{0,4},{8,12},{4,0},{12,8},{1,5},{9,13},{5,1},{13,9},{2,6},{10,14},... | collective-permute-start | bytes 110600 | tf_op jit(solution)/shard_map/ppermute | solution.py:237
  7.9 1.4 %collective-permute-done.refs_1_.refs_5_ = f32[72,128]{1,0:T(8,128)S(1)} collective-permute-done((f32[72,128]{1,0:T(8,128)S(1)}, f32[72,128]{1,0:T(8,128)S(1)}, u32[]{:S(2)}, u32[]{:S(2)}) %collective-permute-start) | collective-permute-done | bytes 36896 | tf_op jit(solution)/shard_map/ppermute | solution.py:237
  9.2 0.0 copy-done
  9.2 0.5 %early.1 = (f32[64,64]{1,0:T(8,128)S(1)}, bf16[64,256]{1,0:T(8,128)(2,1)S(1)}, bf16[256,96]{1,0:T(8,128)(2,1)S(1)}, bf16[256,96]{1,0:T(8,128)(2,1)S(1)}, bf16[64,256]{1,0:T(8,128)(2,1)S(1)}) custom-call(s32[1,256]{1,0:T(1,128)S(1)} %bitcast.4, f32[72,128]{1,0:T(8,128)S(1)} %project.1.refs_0_.refs_4_, f32[72,128]{1,0:T(8,128)S(1)} %collective-permute-done.refs_1_.refs_5_), custom_call_target="tpu_custom_call" | custom-call | flops 1000000 | bytes 100000 | tf_op jit(solution)/shard_map/early/pallas_call | solution.py:271
  9.8 1.4 %collective-permute-done.2.refs_7_ = f32[72,128]{1,0:T(8,128)S(1)} collective-permute-done((f32[72,128]{1,0:T(8,128)S(1)}, f32[72,128]{1,0:T(8,128)S(1)}, u32[]{:S(2)}, u32[]{:S(2)}) %collective-permute-start.2) | collective-permute-done | bytes 36896 | tf_op jit(solution)/shard_map/ppermute | solution.py:237
  11.2 0.4 collective-permute-done.1.refs_6_
  11.5 24.2 %solve.1.a_ref = f32[16,64]{1,0:T(8,128)S(1)} custom-call(f32[64,64]{1,0:T(8,128)S(1)} %get-tuple-element.10.refs_0_, bf16[256,96]{1,0:T(8,128)(2,1)S(1)} %get-tuple-element.11.refs_1_, bf16[256,96]{1,0:T(8,128)(2,1)S(1)} %get-tuple-element.12.refs_2_, bf16[64,256]{1,0:T(8,128)(2,1)S(1)} %get-tuple-element.13.refs_3_, f32[72,128]{1,0:T(8,128)S(1)} %project.1.refs_0_.refs_4_, ...), custom_call_target="tpu_custom_call" | custom-call | tf_op jit(solution)/shard_map/solve/pallas_call | solution.py:280
  35.7 0.1 collective-permute-start.5
  35.8 1.6 %collective-permute-start.4 = (f32[16,64]{1,0:T(8,128)S(1)}, f32[16,64]{1,0:T(8,128)S(1)}, u32[]{:S(2)}, u32[]{:S(2)}) collective-permute-start(f32[16,64]{1,0:T(8,128)S(1)} %solve.1.a_ref), channel_id=1, source_target_pairs={{0,2},{1,3},{2,0},{3,1},{4,6},{5,7},{6,4},{7,5},{8,10},{9,11},{10,... | collective-permute-start | bytes 12296 | tf_op jit(solution)/shard_map/ppermute | solution.py:241
  37.4 0.3 collective-permute-start.3
  37.7 1.3 %collective-permute-done.5.d_ref = f32[16,64]{1,0:T(8,128)S(1)} collective-permute-done((f32[16,64]{1,0:T(8,128)S(1)}, f32[16,64]{1,0:T(8,128)S(1)}, u32[]{:S(2)}, u32[]{:S(2)}) %collective-permute-start.5) | collective-permute-done | bytes 4128 | tf_op jit(solution)/shard_map/ppermute | solution.py:241
  38.9 0.6 %collective-permute-done.4.c_ref = f32[16,64]{1,0:T(8,128)S(1)} collective-permute-done((f32[16,64]{1,0:T(8,128)S(1)}, f32[16,64]{1,0:T(8,128)S(1)}, u32[]{:S(2)}, u32[]{:S(2)}) %collective-permute-start.4) | collective-permute-done | bytes 4128 | tf_op jit(solution)/shard_map/ppermute | solution.py:241
  39.5 0.0 collective-permute-done.3.b_ref
  39.5 0.7 %score.1 = f32[16,256]{1,0:T(8,128)} custom-call(f32[16,64]{1,0:T(8,128)S(1)} %solve.1.a_ref, f32[16,64]{1,0:T(8,128)S(1)} %collective-permute-done.3.b_ref, f32[16,64]{1,0:T(8,128)S(1)} %collective-permute-done.4.c_ref, f32[16,64]{1,0:T(8,128)S(1)} %collective-permute-done.5.d_ref, bf16[64,256]{1,0:T(8,128)(2,1)S(1)} %get-tuple-element.14.chosen_ref), custom_call_target="tpu_custom_call" | custom-call | tf_op jit(solution)/shard_map/score/pallas_call | solution.py:290
Async XLA Ops:
  0.0 9.2 %copy-start = (s32[256]{0:T(256)S(1)}, s32[256]{0:T(256)}, u32[]{:S(2)}) copy-start(s32[256]{0:T(256)} %param.11) | copy-start | bytes 3076
  2.2 7.0 %collective-permute-start = (f32[72,128]{1,0:T(8,128)S(1)}, f32[72,128]{1,0:T(8,128)S(1)}, u32[]{:S(2)}, u32[]{:S(2)}) collective-permute-start(f32[72,128]{1,0:T(8,128)S(1)} %project.1.refs_0_.refs_4_), channel_id=1, source_target_pairs={{0,8},{8,4},{4,12},{12,0},{1,9},{9,5},{5,13},{13,1},{2,10},{10,6},... | collective-permute-start | bytes 110600 | tf_op jit(solution)/shard_map/ppermute | solution.py:237
  6.3 4.9 %collective-permute-start.2 = (f32[72,128]{1,0:T(8,128)S(1)}, f32[72,128]{1,0:T(8,128)S(1)}, u32[]{:S(2)}, u32[]{:S(2)}) collective-permute-start(f32[72,128]{1,0:T(8,128)S(1)} %project.1.refs_0_.refs_4_), channel_id=1, source_target_pairs={{0,12},{8,0},{4,8},{12,4},{1,13},{9,1},{5,9},{13,5},{2,14},{10,2},... | collective-permute-start | bytes 110600 | tf_op jit(solution)/shard_map/ppermute | solution.py:237
  7.4 4.2 %collective-permute-start.1 = (f32[72,128]{1,0:T(8,128)S(1)}, f32[72,128]{1,0:T(8,128)S(1)}, u32[]{:S(2)}, u32[]{:S(2)}) collective-permute-start(f32[72,128]{1,0:T(8,128)S(1)} %project.1.refs_0_.refs_4_), channel_id=1, source_target_pairs={{0,4},{8,12},{4,0},{12,8},{1,5},{9,13},{5,1},{13,9},{2,6},{10,14},... | collective-permute-start | bytes 110600 | tf_op jit(solution)/shard_map/ppermute | solution.py:237
  35.7 3.2 %collective-permute-start.5 = (f32[16,64]{1,0:T(8,128)S(1)}, f32[16,64]{1,0:T(8,128)S(1)}, u32[]{:S(2)}, u32[]{:S(2)}) collective-permute-start(f32[16,64]{1,0:T(8,128)S(1)} %solve.1.a_ref), channel_id=1, source_target_pairs={{0,3},{1,2},{2,1},{3,0},{4,7},{5,6},{6,5},{7,4},{8,11},{9,10},{10,... | collective-permute-start | bytes 12296 | tf_op jit(solution)/shard_map/ppermute | solution.py:241
  35.8 3.7 %collective-permute-start.4 = (f32[16,64]{1,0:T(8,128)S(1)}, f32[16,64]{1,0:T(8,128)S(1)}, u32[]{:S(2)}, u32[]{:S(2)}) collective-permute-start(f32[16,64]{1,0:T(8,128)S(1)} %solve.1.a_ref), channel_id=1, source_target_pairs={{0,2},{1,3},{2,0},{3,1},{4,6},{5,7},{6,4},{7,5},{8,10},{9,11},{10,... | collective-permute-start | bytes 12296 | tf_op jit(solution)/shard_map/ppermute | solution.py:241
  37.4 2.2 %collective-permute-start.3 = (f32[16,64]{1,0:T(8,128)S(1)}, f32[16,64]{1,0:T(8,128)S(1)}, u32[]{:S(2)}, u32[]{:S(2)}) collective-permute-start(f32[16,64]{1,0:T(8,128)S(1)} %solve.1.a_ref), channel_id=1, source_target_pairs={{0,1},{1,0},{2,3},{3,2},{4,5},{5,4},{6,7},{7,6},{8,9},{9,8},{10,11... | collective-permute-start | bytes 12296 | tf_op jit(solution)/shard_map/ppermute | solution.py:241
